TPU v7x, 128 devices: a whole 4x4x4 slice. The times are simulated.
128 devices in a mesh: ctx: 32 (over z_lo, y, x), fsdp: 4 (over z_hi, core).
Axes of the slice: x: 4, y: 4, z: 4 (z_hi: 2, z_lo: 2; z = z_hi * 2 + z_lo), core: 2. Of those that a mesh axis runs over, the one named last changes fastest.
Arguments:
- tokens: bfloat16 [4, 4096, 1024], P('fsdp', 'ctx'), may hold values from -6 to 6
- query_weight: bfloat16 [1024, 2048], P('fsdp'), may hold values from -0.1875 to 0.1875
- key_weight: bfloat16 [1024, 1024], P('fsdp'), may hold values from -0.1875 to 0.1875
- value_weight: bfloat16 [1024, 1024], P('fsdp'), may hold values from -0.1875 to 0.1875
- out_weight: bfloat16 [1024, 2048], P('fsdp'), may hold values from -3 to 3
- gate_weight: bfloat16 [1024, 3072], P('fsdp'), may hold values from -0.1875 to 0.1875
- up_weight: bfloat16 [1024, 3072], P('fsdp'), may hold values from -0.1875 to 0.1875
- down_weight: bfloat16 [1024, 3072], P('fsdp'), may hold values from -0.21875 to 0.21875
- attn_gain: float32 [1024], replicated, may hold values from 0.5 to 1.5
- mlp_gain: float32 [1024], replicated, may hold values from 0.5 to 1.5
- query_gain: float32 [128], replicated, may hold values from 1 to 1.6
- key_gain: float32 [128], replicated, may hold values from 1 to 1.6
- pair_order: int32 [4, 32], P('fsdp'), may hold values from 0 to 31, each once within a row
- out_grad: bfloat16 [4, 4096, 1024], P('fsdp', 'ctx'), may hold values from -6 to 6
Outputs:
- output: bfloat16 [4, 4096, 1024], P('fsdp', 'ctx')
- input_grad: float32 [4, 4096, 1024], P('fsdp', 'ctx')
- query_weight_grad: float32 [1024, 2048], P('fsdp')
- key_weight_grad: float32 [1024, 1024], P('fsdp')
- value_weight_grad: float32 [1024, 1024], P('fsdp')
- out_weight_grad: float32 [1024, 2048], P('fsdp')
- gate_weight_grad: float32 [1024, 3072], P('fsdp')
- up_weight_grad: float32 [1024, 3072], P('fsdp')
- down_weight_grad: float32 [1024, 3072], P('fsdp')
- attn_gain_grad: float32 [1024], replicated
- mlp_gain_grad: float32 [1024], replicated
- query_gain_grad: float32 [128], replicated
- key_gain_grad: float32 [128], replicated
Inputs may be any that keep to these rules, and one draw needn't show every extreme that they name: Each row is a permutation of 0 to 31; device c of the context axis holds blocks pair_order[s, c] and 63 - pair_order[s, c] of sequence s, each of 64 tokens, in that order.
All inputs are finite; a program needn't handle non-finite values.
Results may differ from a plain program's by a relative error of at most 0.035.
Values may be sent and summed in bfloat16 or wider, within the bound.
A program may use at most 256 MiB of HBM per device.

v0:
```python
import jax
import jax.numpy as jnp
from jax import lax
from jax.sharding import PartitionSpec as P

EPSILON = 1e-06
ROPE_BASE = 1000000.0
MASKED = -1e30


def token_positions(pair_row, row_index, half_len, ctx_count):
    owner_dev = row_index // (2 * half_len)
    inner_row = row_index % (2 * half_len)
    matches = owner_dev[:, None] == jnp.arange(ctx_count, dtype=jnp.int32)[None, :]
    first_block = jnp.sum(jnp.where(matches, pair_row[None, :], 0), axis=1)
    block_index = jnp.where(inner_row < half_len, first_block, 2 * ctx_count - 1 - first_block)
    return block_index * half_len + inner_row % half_len


def rms_scale(values):
    return lax.rsqrt(jnp.mean(values * values, axis=-1, keepdims=True) + EPSILON)


def rope_tables(extent, positions):
    frequency = jnp.power(ROPE_BASE, -jnp.arange(0, extent, 2, dtype=jnp.float32) / extent)
    angles = positions.astype(jnp.float32)[:, None] * frequency[None, :]
    cosine = jnp.concatenate([jnp.cos(angles), jnp.cos(angles)], -1)[:, None, :]
    sine_rows = jnp.concatenate([jnp.sin(angles), jnp.sin(angles)], -1)[:, None, :]
    return (cosine, sine_rows)


def rotate(values, positions):
    extent = values.shape[-1]
    cosine, sine_rows = rope_tables(extent, positions)
    lower_half = values[..., : extent // 2]
    upper_half = values[..., extent // 2 :]
    return values * cosine + jnp.concatenate([-upper_half, lower_half], -1) * sine_rows


def rotate_back(grad_rows, positions):
    extent = grad_rows.shape[-1]
    cosine, sine_rows = rope_tables(extent, positions)
    scaled = grad_rows * sine_rows
    return grad_rows * cosine + jnp.concatenate(
        [scaled[..., extent // 2 :], -scaled[..., : extent // 2]], -1
    )


def norm_back(grad_out, normed, scale_inv):
    return scale_inv * (grad_out - normed * jnp.mean(grad_out * normed, axis=-1, keepdims=True))


def matmul_rows(matrix, second):
    return lax.dot_general(
        matrix, second, (((1,), (1,)), ((), ())), preferred_element_type=jnp.float32
    )


def matmul_cols(matrix, second):
    return lax.dot_general(
        matrix, second, (((0,), (0,)), ((), ())), preferred_element_type=jnp.float32
    )


def shards(
    tokens,
    query_weight,
    key_weight,
    value_weight,
    out_weight,
    gate_weight,
    up_weight,
    down_weight,
    attn_gain,
    mlp_gain,
    query_gain,
    key_gain,
    pair_order,
    out_grad,
):
    inputs = tokens[0].astype(jnp.float32)
    local_rows = inputs.shape[0]
    half_len = local_rows // 2
    ctx_count = lax.axis_size("ctx")
    seq_len = local_rows * ctx_count
    head_dim = query_gain.shape[0]
    pair_row = pair_order[0]
    own_index = lax.axis_index("ctx") * local_rows + jnp.arange(local_rows, dtype=jnp.int32)
    own_pos = token_positions(pair_row, own_index, half_len, ctx_count)
    full_query, full_key, full_value, full_out, full_gate, full_up, full_down = (
        lax.all_gather(query_weight, "fsdp", axis=0, tiled=True),
        lax.all_gather(key_weight, "fsdp", axis=0, tiled=True),
        lax.all_gather(value_weight, "fsdp", axis=0, tiled=True),
        lax.all_gather(out_weight, "fsdp", axis=0, tiled=True),
        lax.all_gather(gate_weight, "fsdp", axis=0, tiled=True),
        lax.all_gather(up_weight, "fsdp", axis=0, tiled=True),
        lax.all_gather(down_weight, "fsdp", axis=0, tiled=True),
    )
    head_count = full_query.shape[1] // head_dim
    kv_heads = full_key.shape[1] // head_dim
    group_size = head_count // kv_heads
    query_cols = head_count * head_dim
    key_cols = kv_heads * head_dim
    ff_count = full_gate.shape[1]
    score_scale = head_dim ** (-0.5)
    key_block = min(512, seq_len)
    block_count = seq_len // key_block
    attn_scale = rms_scale(inputs)
    attn_normed = inputs * attn_scale
    attn_in = (attn_normed * attn_gain).astype(jnp.bfloat16)
    query_raw = jnp.dot(attn_in, full_query, preferred_element_type=jnp.float32).reshape(
        local_rows, head_count, head_dim
    )
    key_raw = jnp.dot(attn_in, full_key, preferred_element_type=jnp.float32).reshape(
        local_rows, kv_heads, head_dim
    )
    value_rows = jnp.dot(attn_in, full_value, preferred_element_type=jnp.float32).astype(
        jnp.bfloat16
    )
    query_inv = rms_scale(query_raw)
    query_hat = query_raw * query_inv
    key_inv = rms_scale(key_raw)
    key_hat = key_raw * key_inv
    query_rot = (
        rotate(query_hat * query_gain, own_pos)
        .astype(jnp.bfloat16)
        .reshape(local_rows, kv_heads, group_size, head_dim)
    )
    key_rot = rotate(key_hat * key_gain, own_pos).astype(jnp.bfloat16).reshape(local_rows, key_cols)
    keys_all, values_all = (
        lax.all_gather(key_rot, "ctx", axis=0, tiled=True),
        lax.all_gather(value_rows, "ctx", axis=0, tiled=True),
    )
    key_blocks = keys_all.reshape(block_count, key_block, kv_heads, head_dim)
    value_blocks = values_all.reshape(block_count, key_block, kv_heads, head_dim)
    key_pos = token_positions(
        pair_row, jnp.arange(seq_len, dtype=jnp.int32), half_len, ctx_count
    ).reshape(block_count, key_block)

    def block_scores(key_part, pos_part):
        scores = (
            jnp.einsum("qkgd,tkd->kgqt", query_rot, key_part, preferred_element_type=jnp.float32)
            * score_scale
        )
        allowed = own_pos[:, None] >= pos_part[None, :]
        return (jnp.where(allowed, scores, MASKED), allowed)

    def peak_step(carry_state, block_in):
        row_peak, denominator = carry_state
        key_part, pos_part = block_in
        scores, allowed = block_scores(key_part, pos_part)
        new_peak = jnp.maximum(row_peak, jnp.max(scores, axis=-1, keepdims=True))
        block_sum = jnp.sum(
            jnp.where(allowed, jnp.exp(scores - new_peak), 0.0), axis=-1, keepdims=True
        )
        return ((new_peak, denominator * jnp.exp(row_peak - new_peak) + block_sum), None)

    stat_shape = (kv_heads, group_size, local_rows, 1)
    (row_peak, denominator), unused = lax.scan(
        peak_step,
        (jnp.full(stat_shape, MASKED, jnp.float32), jnp.zeros(stat_shape, jnp.float32)),
        (key_blocks, key_pos),
    )
    log_total = row_peak + jnp.log(denominator)

    def mix_step(accumulated, block_in):
        key_part, value_part, pos_part = block_in
        scores, allowed = block_scores(key_part, pos_part)
        prob_rows = jnp.where(allowed, jnp.exp(scores - log_total), 0.0).astype(jnp.bfloat16)
        return (
            accumulated
            + jnp.einsum(
                "kgqt,tkd->qkgd", prob_rows, value_part, preferred_element_type=jnp.float32
            ),
            None,
        )

    attended, unused = lax.scan(
        mix_step,
        jnp.zeros((local_rows, kv_heads, group_size, head_dim), jnp.float32),
        (key_blocks, value_blocks, key_pos),
    )
    attn_out = attended.reshape(local_rows, query_cols).astype(jnp.bfloat16)
    middle = inputs + matmul_rows(attn_out, full_out)
    mlp_scale = rms_scale(middle)
    mlp_normed = middle * mlp_scale
    mlp_in = (mlp_normed * mlp_gain).astype(jnp.bfloat16)
    gate_pre = jnp.dot(mlp_in, full_gate, preferred_element_type=jnp.float32)
    up_pre = jnp.dot(mlp_in, full_up, preferred_element_type=jnp.float32)
    sigmoid_gate = jax.nn.sigmoid(gate_pre)
    silu_gate = gate_pre * sigmoid_gate
    hidden = (silu_gate * up_pre).astype(jnp.bfloat16)
    result = middle + matmul_rows(hidden, full_down)
    out_cot = out_grad[0].astype(jnp.float32)
    down_cot = out_grad[0]
    hidden_cot = jnp.dot(down_cot, full_down, preferred_element_type=jnp.float32)
    gate_cot = (
        hidden_cot * up_pre * sigmoid_gate * (1.0 + gate_pre * (1.0 - sigmoid_gate))
    ).astype(jnp.bfloat16)
    up_cot = (hidden_cot * silu_gate).astype(jnp.bfloat16)
    gate_up_cot = jnp.concatenate([gate_cot, up_cot], 1)
    mlp_sum = lax.psum_scatter(
        jnp.concatenate(
            [matmul_cols(mlp_in, gate_up_cot), matmul_cols(down_cot, hidden)], 1
        ).astype(jnp.bfloat16),
        "fsdp",
        scatter_dimension=0,
        tiled=True,
    ).astype(jnp.float32)
    mlp_in_cot = matmul_rows(gate_cot, full_gate) + matmul_rows(up_cot, full_up)
    mlp_gain_part = jnp.sum(mlp_in_cot * mlp_normed, axis=0)
    middle_cot = out_cot + norm_back(mlp_in_cot * mlp_gain, mlp_normed, mlp_scale)
    branch_cot = middle_cot.astype(jnp.bfloat16)
    attended_cot = (
        jnp.dot(branch_cot, full_out, preferred_element_type=jnp.float32)
        .astype(jnp.bfloat16)
        .reshape(local_rows, kv_heads, group_size, head_dim)
    )
    delta_rows = jnp.sum(attended_cot.astype(jnp.float32) * attended, axis=-1).transpose(1, 2, 0)[
        ..., None
    ]

    def grad_step(query_cot, block_in):
        key_part, value_part, pos_part = block_in
        scores, allowed = block_scores(key_part, pos_part)
        prob_rows = jnp.where(allowed, jnp.exp(scores - log_total), 0.0)
        prob_cot = jnp.einsum(
            "qkgd,tkd->kgqt", attended_cot, value_part, preferred_element_type=jnp.float32
        )
        score_cot = (prob_rows * (prob_cot - delta_rows)).astype(jnp.bfloat16)
        query_cot = query_cot + jnp.einsum(
            "kgqt,tkd->qkgd", score_cot, key_part, preferred_element_type=jnp.float32
        )
        key_part_cot = jnp.einsum(
            "kgqt,qkgd->tkd", score_cot, query_rot, preferred_element_type=jnp.float32
        )
        value_part_cot = jnp.einsum(
            "kgqt,qkgd->tkd",
            prob_rows.astype(jnp.bfloat16),
            attended_cot,
            preferred_element_type=jnp.float32,
        )
        return (query_cot, (key_part_cot, value_part_cot))

    query_cot, (key_cots, value_cots) = lax.scan(
        grad_step,
        jnp.zeros((local_rows, kv_heads, group_size, head_dim), jnp.float32),
        (key_blocks, value_blocks, key_pos),
    )
    own_key_cot, own_value_cot = (
        lax.psum_scatter(
            (key_cots.reshape(seq_len, key_cols) * score_scale).astype(jnp.bfloat16),
            "ctx",
            scatter_dimension=0,
            tiled=True,
        ).astype(jnp.float32),
        lax.psum_scatter(
            value_cots.reshape(seq_len, key_cols).astype(jnp.bfloat16),
            "ctx",
            scatter_dimension=0,
            tiled=True,
        ).astype(jnp.float32),
    )
    value_raw_cot = own_value_cot.astype(jnp.bfloat16)
    key_rot_cot = rotate_back(own_key_cot.reshape(local_rows, kv_heads, head_dim), own_pos)
    key_gain_part = jnp.sum(key_rot_cot * key_hat, axis=(0, 1))
    key_raw_cot = (
        norm_back(key_rot_cot * key_gain, key_hat, key_inv)
        .astype(jnp.bfloat16)
        .reshape(local_rows, key_cols)
    )
    query_rot_cot = rotate_back(
        (query_cot * score_scale).reshape(local_rows, head_count, head_dim), own_pos
    )
    query_gain_part = jnp.sum(query_rot_cot * query_hat, axis=(0, 1))
    query_raw_cot = (
        norm_back(query_rot_cot * query_gain, query_hat, query_inv)
        .astype(jnp.bfloat16)
        .reshape(local_rows, query_cols)
    )
    proj_cot = jnp.concatenate([query_raw_cot, key_raw_cot, value_raw_cot], 1)
    attn_sum = lax.psum_scatter(
        jnp.concatenate(
            [matmul_cols(attn_in, proj_cot), matmul_cols(branch_cot, attn_out)], 1
        ).astype(jnp.bfloat16),
        "fsdp",
        scatter_dimension=0,
        tiled=True,
    ).astype(jnp.float32)
    attn_in_cot = (
        matmul_rows(query_raw_cot, full_query)
        + matmul_rows(key_raw_cot, full_key)
        + matmul_rows(value_raw_cot, full_value)
    )
    attn_gain_part = jnp.sum(attn_in_cot * attn_normed, axis=0)
    input_cot = middle_cot + norm_back(attn_in_cot * attn_gain, attn_normed, attn_scale)
    gain_totals = lax.psum(
        (attn_gain_part, mlp_gain_part, query_gain_part, key_gain_part), ("ctx", "fsdp")
    )
    mlp_sum, attn_sum = (
        lax.psum(mlp_sum.astype(jnp.bfloat16), "ctx").astype(jnp.float32),
        lax.psum(attn_sum.astype(jnp.bfloat16), "ctx").astype(jnp.float32),
    )
    return (
        result.astype(jnp.bfloat16)[None],
        input_cot[None],
        attn_sum[:, :query_cols],
        attn_sum[:, query_cols : query_cols + key_cols],
        attn_sum[:, query_cols + key_cols : query_cols + 2 * key_cols],
        attn_sum[:, query_cols + 2 * key_cols :],
        mlp_sum[:, :ff_count],
        mlp_sum[:, ff_count : 2 * ff_count],
        mlp_sum[:, 2 * ff_count :],
        gain_totals[0],
        gain_totals[1],
        gain_totals[2],
        gain_totals[3],
    )


def solution(mesh):
    placed = (
        P("fsdp", "ctx", None),
        P("fsdp", None),
        P("fsdp", None),
        P("fsdp", None),
        P("fsdp", None),
        P("fsdp", None),
        P("fsdp", None),
        P("fsdp", None),
        P(),
        P(),
        P(),
        P(),
        P("fsdp", None),
        P("fsdp", "ctx", None),
    )
    return jax.shard_map(
        shards,
        mesh=mesh,
        in_specs=placed,
        out_specs=(
            P("fsdp", "ctx", None),
            P("fsdp", "ctx", None),
            P("fsdp", None),
            P("fsdp", None),
            P("fsdp", None),
            P("fsdp", None),
            P("fsdp", None),
            P("fsdp", None),
            P("fsdp", None),
            P(),
            P(),
            P(),
            P(),
        ),
        check_vma=False,
    )
```

profile of v0, /device:TPU:0, one launch (start us, length us, event | category | flops | bytes accessed | tf_op | source)
XLA Modules:
  0.0 1768.5 jit_solution(12505794464127278058)
XLA Ops:
  10.6 28.4 %all-gather.10.cloned.1.call-done = bf16[1024,1024]{1,0:T(8,128)(2,1)} async-done(((bf16[256,1024]{1,0:T(8,128)(2,1)}), bf16[1024,1024]{1,0:T(8,128)(2,1)}) %all-gather.10.cloned.1.call-update) | async-done | bytes 2097168 | tf_op jit(solution)/shard_map/all_gather | solution.py:93
  42.3 24.3 %all-gather.14.cloned.1.call-done = bf16[1024,1024]{1,0:T(8,128)(2,1)} async-done(((bf16[256,1024]{1,0:T(8,128)(2,1)}), bf16[1024,1024]{1,0:T(8,128)(2,1)}) %all-gather.14.cloned.1.call-update) | async-done | bytes 2097168 | tf_op jit(solution)/shard_map/all_gather | solution.py:92
  75.3 30.9 %all-gather.18.cloned.1.call-done = bf16[1024,2048]{1,0:T(8,128)(2,1)} async-done(((bf16[256,2048]{1,0:T(8,128)(2,1)}), bf16[1024,2048]{1,0:T(8,128)(2,1)}) %all-gather.18.cloned.1.call-update) | async-done | bytes 4194320 | tf_op jit(solution)/shard_map/all_gather | solution.py:91
  106.2 6.7 copy.64
  112.9 3.6 multiply_reduce_fusion.3
  117.7 156.7 %all-gather.12.cloned.1.call-done = bf16[4096,1024]{1,0:T(8,128)(2,1)} async-done(((bf16[128,1024]{1,0:T(8,128)(2,1)}), bf16[4096,1024]{1,0:T(8,128)(2,1)}) %all-gather.12.cloned.1.call-update) | async-done | bytes 8388624 | tf_op jit(solution)/shard_map/all_gather | solution.py:132
  274.5 8.8 copy.95
  283.3 161.5 %all-gather.16.cloned.1.call-done = bf16[4096,1024]{1,0:T(8,128)(2,1)} async-done(((bf16[128,1024]{1,0:T(8,128)(2,1)}), bf16[4096,1024]{1,0:T(8,128)(2,1)}) %all-gather.16.cloned.1.call-update) | async-done | bytes 8388624 | tf_op jit(solution)/shard_map/all_gather | solution.py:131
  444.8 8.8 copy.96
  453.6 9.2 copy.68
  462.8 59.6 %while.39 = (s32[]{:T(128)}, f32[8,2,128,1]{2,1,0,3:T(2,128)S(1)}, f32[8,2,128,1]{2,1,0,3:T(2,128)S(1)}, s32[128]{0:T(128)S(1)}, s32[8,512]{1,0:T(8,128)S(1)}, /...) while((s32[]{:T(128)}, f32[8,2,128,1]{2,1,0,3:T(2,128)S(1)}, ...), condition=%wide.region_8.9_spmd.clone, body=%wide.region_5.8_spmd.clone.sunk | while | flops 276899840 | bytes 10271352 | solution.py:159
  463.0 3.9 fusion.168
  470.3 3.9 fusion.168
  477.7 3.9 fusion.168
  481.6 3.2 select_reduce_fusion.4
  485.1 4.0 fusion.168
  492.5 3.9 fusion.168
  496.4 3.7 select_reduce_fusion.4
  500.4 4.0 fusion.168
  507.8 3.9 fusion.168
  515.2 3.9 fusion.168
  519.1 3.2 select_reduce_fusion.4
  522.4 49.4 %while.40 = (s32[]{:T(128)}, f32[128,8,2,128]{0,3,2,1:T(8,128)}, bf16[8,512,8,128]{3,2,1,0:T(8,128)(2,1)}, s32[128]{0:T(128)S(1)}, s32[8,512]{1,0:T(8,128)S(1)},...) while((s32[]{:T(128)}, f32[128,8,2,128]{0,3,2,1:T(8,128)}, ...), condition=%wide.region_10.11_spmd.clone, body=%wide.region_9.10_spmd.clone.sunk | while | flops 542703616 | bytes 9058947 | solution.py:178
  524.6 3.6 fusion.172
  530.4 4.0 fusion.172
  536.5 4.0 fusion.172
  542.7 4.0 fusion.172
  548.9 4.2 fusion.172
  555.2 4.0 fusion.172
  561.3 4.0 fusion.172
  567.4 3.9 fusion.172
  573.2 4.0 multiply_reduce_fusion.8
  577.4 5.0 fusion.110
  582.4 6.9 all-gather.24.cloned.1.call-done
  589.3 4.9 fusion.111
  594.2 46.6 %all-gather.26.cloned.1.call-done = bf16[1024,3072]{1,0:T(8,128)(2,1)} async-done(((bf16[256,3072]{1,0:T(8,128)(2,1)}), bf16[1024,3072]{1,0:T(8,128)(2,1)}) %all-gather.26.cloned.1.call-update) | async-done | bytes 6291472 | tf_op jit(solution)/shard_map/all_gather | solution.py:97
  640.7 6.3 multiply_convert_fusion.1
  647.0 5.6 fusion.112
  661.6 105.1 %while.41 = (s32[]{:T(128)}, f32[128,8,2,128]{0,3,2,1:T(8,128)}, f32[8,512,8,128]{3,1,2,0:T(8,128)}, bf16[8,512,8,128]{3,1,2,0:T(8,128)(2,1)}, bf16[8,512,8,128]...) while((s32[]{:T(128)}, f32[128,8,2,128]{0,3,2,1:T(8,128)}, ...), condition=%wide.region_15.16_spmd.clone, body=%wide.region_14.15_spmd.clone.sunk | while | flops 1355350016 | bytes 70482712 | solution.py:245
  680.5 3.2 fusion.184
  693.6 3.2 fusion.184
  720.0 3.2 fusion.184
  733.1 3.2 fusion.184
  746.3 3.2 fusion.184
  759.4 3.2 fusion.184
  766.7 9.6 multiply_convert_fusion
  776.3 12.1 copy.75
  788.4 8.9 copy.104
  797.6 12.1 copy.77
  809.7 8.9 copy.103
  819.8 4.5 convert_bitcast_fusion
  824.2 5.1 convolution_convert_fusion
  829.3 16.2 pad_maximum_fusion
  849.2 3.3 convolution_convert_fusion.2
  852.5 123.8 %reduce-scatter.5.cloned.1.call-done = bf16[128,1024]{1,0:T(8,128)(2,1)} async-done(((bf16[4096,1024]{1,0:T(8,128)(2,1)}), bf16[128,1024]{1,0:T(8,128)(2,1)}) %reduce-scatter.5.cloned.1.call-update) | async-done | bytes 262160 | tf_op jit(solution)/shard_map/reduce_scatter | solution.py:251
  977.4 176.0 %reduce-scatter.7.cloned.1.call-done = bf16[128,1024]{1,0:T(8,128)(2,1)} async-done(((bf16[4096,1024]{1,0:T(8,128)(2,1)}), bf16[128,1024]{1,0:T(8,128)(2,1)}) %reduce-scatter.7.cloned.1.call-update) | async-done | bytes 262160 | tf_op jit(solution)/shard_map/reduce_scatter | solution.py:257
  1158.9 9.0 pad_maximum_fusion.1
  1168.2 131.4 %reduce-scatter.11.cloned.1.call-done = bf16[256,9216]{1,0:T(8,128)(2,1)} async-done(((bf16[1024,9216]{1,0:T(8,128)(2,1)}), bf16[256,9216]{1,0:T(8,128)(2,1)}) %reduce-scatter.11.cloned.1.call-update) | async-done | bytes 4718608 | tf_op jit(solution)/shard_map/reduce_scatter | solution.py:202
  1299.6 108.3 %reduce-scatter.9.cloned.1.call-done = bf16[256,6144]{1,0:T(8,128)(2,1)} async-done(((bf16[1024,6144]{1,0:T(8,128)(2,1)}), bf16[256,6144]{1,0:T(8,128)(2,1)}) %reduce-scatter.9.cloned.1.call-update) | async-done | bytes 3145744 | tf_op jit(solution)/shard_map/reduce_scatter | solution.py:282
  1407.9 5.8 fusion.54
  1417.7 68.6 %all-reduce = (f32[1024]{0:T(1024)}, f32[1024]{0:T(1024)}, f32[128]{0:T(128)}, f32[128]{0:T(128)}) all-reduce(f32[1024]{0:T(1024)S(1)} %get-tuple-element.340, f32[1024]{0:T(1024)S(1)} %get-tuple-element.338, f32[128]{0:T(128)S(1)} %copy-done.48, f32[128]{0:T(128)S(1)} %get-tuple-element.336), channel_id=1, replica_groups=mesh['ctx'=32,'fsdp'=4] {'ctx','fsdp'}, use_global_device_ids=true, to_apply=%region_26.27 | all-reduce | flops 2304 | bytes 18432 | tf_op jit(solution)/shard_map/psum | solution.py:297
  1487.3 264.5 %all-reduce.4.cloned.1.call-done = (bf16[256,6144]{1,0:T(8,128)(2,1)}, bf16[256,9216]{1,0:T(8,128)(2,1)}) async-done(((bf16[256,6144]{1,0:T(8,128)(2,1)}, bf16[256,9216]{1,0:T(8,128)(2,1)}), (bf16[256,6144]{1,0:T(8,128)(2,1)}, bf16[256,9216]{1,0:T(8,128)(2,1)})) %all-reduce.4.cloned.1.call-update) | async-done | bytes 7864336 | tf_op jit(solution)/shard_map/psum | solution.py:302
  1751.8 4.4 fusion.106
  1757.7 4.1 fusion.105
  (389 shorter events, 164.4 us)
Async XLA Ops:
  7.2 34.8 %copy-start.49 = (s32[1,32]{1,0:T(1,128)S(1)}, s32[1,32]{1,0:T(1,128)}, u32[]{:S(2)}) copy-start(s32[1,32]{1,0:T(1,128)} %param.32) | copy-start | bytes 388
  7.2 31.8 %all-gather.10.cloned.1.call-start = ((), (), s32[]{:S(2)}) async-start(), calls=%async_computation.4 | async-start | bytes 2621440 | tf_op jit(solution)/shard_map/all_gather | solution.py:93
  7.9 58.7 %all-gather.14.cloned.1.call-start = ((), (), s32[]{:S(2)}) async-start(), calls=%async_computation.6 | async-start | bytes 2621440 | tf_op jit(solution)/shard_map/all_gather | solution.py:92
  8.7 60.8 %copy-start.6 = (bf16[1,128,1024]{2,1,0:T(8,128)(2,1)S(1)}, bf16[1,128,1024]{2,1,0:T(8,128)(2,1)}, u32[]{:S(2)}) copy-start(bf16[1,128,1024]{2,1,0:T(8,128)(2,1)} %param.20) | copy-start | bytes 786436
  8.7 60.8 %copy-start.36 = (f32[1024]{0:T(1024)S(1)}, f32[1024]{0:T(1024)}, u32[]{:S(2)}) copy-start(f32[1024]{0:T(1024)} %param.28) | copy-start | bytes 12292
  8.7 97.5 %all-gather.18.cloned.1.call-start = ((), (), s32[]{:S(2)}) async-start(), calls=%async_computation.8 | async-start | bytes 5242880 | tf_op jit(solution)/shard_map/all_gather | solution.py:91
  9.4 265.0 %all-gather.12.cloned.1.call-start = ((), (), s32[]{:S(2)}) async-start(), calls=%async_computation.5 | async-start | bytes 8650752 | tf_op jit(solution)/shard_map/all_gather | solution.py:132
  10.6 102.3 %copy-start.43 = (f32[128]{0:T(128)}, f32[128]{0:T(128)S(1)}, u32[]{:S(2)}) copy-start(f32[128]{0:T(128)S(1)} %add_rsqrt_fusion.3) | copy-start | bytes 1540
  41.9 28.5 %copy-start.47 = (f32[128]{0:T(128)S(1)}, f32[128]{0:T(128)}, u32[]{:S(2)}) copy-start(f32[128]{0:T(128)} %param.31) | copy-start | bytes 1540
  41.9 402.9 %all-gather.16.cloned.1.call-start = ((), (), s32[]{:S(2)}) async-start(), calls=%async_computation.7 | async-start | bytes 8650752 | tf_op jit(solution)/shard_map/all_gather | solution.py:131
  42.3 74.5 %copy-start.27 = (f32[128,128]{0,1:T(8,128)}, f32[128,128]{0,1:T(8,128)S(1)}, u32[]{:S(2)}) copy-start(f32[128,128]{0,1:T(8,128)S(1)} %get-tuple-element.436) | copy-start | bytes 196612
  42.3 74.5 %copy-start.29 = (f32[128,128]{0,1:T(8,128)}, f32[128,128]{0,1:T(8,128)S(1)}, u32[]{:S(2)}) copy-start(f32[128,128]{0,1:T(8,128)S(1)} %get-tuple-element.437) | copy-start | bytes 196612
  72.2 501.1 %all-gather.20.cloned.1.call-start = ((), (), s32[]{:S(2)}) async-start(), calls=%async_computation.9 | async-start | bytes 5242880 | tf_op jit(solution)/shard_map/all_gather | solution.py:94
  72.7 504.6 %all-gather.22.cloned.1.call-start = ((), (), s32[]{:S(2)}) async-start(), calls=%async_computation.10 | async-start | bytes 7864320 | tf_op jit(solution)/shard_map/all_gather | solution.py:95
  73.5 515.8 %all-gather.24.cloned.1.call-start = ((), (), s32[]{:S(2)}) async-start(), calls=%async_computation.11 | async-start | bytes 7864320 | tf_op jit(solution)/shard_map/all_gather | solution.py:96
  74.3 566.5 %all-gather.26.cloned.1.call-start = ((), (), s32[]{:S(2)}) async-start(), calls=%async_computation.12 | async-start | bytes 7864320 | tf_op jit(solution)/shard_map/all_gather | solution.py:97
  75.0 901.3 %reduce-scatter.5.cloned.1.call-start = ((), (), s32[]{:S(2)}) async-start(), calls=%async_computation.13 | async-start | bytes 8650752 | tf_op jit(solution)/shard_map/reduce_scatter | solution.py:251
  116.5 166.8 %copy-start.38 = (f32[128,16]{0,1:T(8,128)}, f32[128,16]{0,1:T(8,128)S(1)}, u32[]{:S(2)}) copy-start(f32[128,16]{0,1:T(8,128)S(1)} %add_rsqrt_fusion) | copy-start | bytes 24580
  571.9 5.3 copy-start.42
  577.3 11.9 copy-start.17
  582.4 58.4 %copy-start.31 = (bf16[1,128,1024]{2,1,0:T(8,128)(2,1)S(1)}, bf16[1,128,1024]{2,1,0:T(8,128)(2,1)}, u32[]{:S(2)}) copy-start(bf16[1,128,1024]{2,1,0:T(8,128)(2,1)} %param.33) | copy-start | bytes 786436
  647.0 5.6 copy-start.25
  647.0 8.1 copy-start.26
  647.0 5.6 copy-start.2
  655.3 5.1 copy-start.13
  655.3 5.1 copy-start.24
  661.8 4.3 copy-start.34
  667.6 5.0 copy-start.1
  667.6 5.0 copy-start.35
  674.6 4.3 copy-start.34
  680.5 5.3 copy-start.1
  680.5 5.3 copy-start.35
  687.7 4.3 copy-start.34
  693.6 5.3 copy-start.1
  693.6 5.3 copy-start.35
  706.8 5.3 copy-start.1
  706.8 5.3 copy-start.35
  720.0 5.2 copy-start.1
  720.0 5.2 copy-start.35
  733.1 5.3 copy-start.1
  733.1 5.3 copy-start.35
  740.5 4.3 copy-start.34
  746.3 5.2 copy-start.1
  746.3 5.2 copy-start.35
  753.6 4.3 copy-start.34
  759.4 5.2 copy-start.1
  759.4 5.2 copy-start.35
  797.4 356.0 %reduce-scatter.7.cloned.1.call-start = ((), (), s32[]{:S(2)}) async-start(), calls=%async_computation.14 | async-start | bytes 8650752 | tf_op jit(solution)/shard_map/reduce_scatter | solution.py:257
  818.6 481.0 %reduce-scatter.11.cloned.1.call-start = ((), (), s32[]{:S(2)}) async-start(), calls=%async_computation.16 | async-start | bytes 23592960 | tf_op jit(solution)/shard_map/reduce_scatter | solution.py:202
  819.8 4.5 copy-start.18
  845.6 562.3 %reduce-scatter.9.cloned.1.call-start = ((), (), s32[]{:S(2)}) async-start(), calls=%async_computation.15 | async-start | bytes 15728640 | tf_op jit(solution)/shard_map/reduce_scatter | solution.py:282
  849.2 305.4 %copy-start.11 = (f32[128,8,128]{0,2,1:T(8,128)S(1)}, f32[128,8,128]{0,2,1:T(8,128)}, u32[]{:S(2)}) copy-start(f32[128,8,128]{0,2,1:T(8,128)} %copy-done.10) | copy-start | bytes 1572868
  849.2 305.4 %copy-start.41 = (f32[128,8]{0,1:T(8,128)S(1)}, f32[128,8]{0,1:T(8,128)}, u32[]{:S(2)}) copy-start(f32[128,8]{0,1:T(8,128)} %copy-done.40) | copy-start | bytes 12292
  852.5 303.8 %copy-start.23 = (bf16[128,16,128]{0,2,1:T(8,128)(2,1)S(1)}, bf16[128,16,128]{0,2,1:T(8,128)(2,1)}, u32[]{:S(2)}) copy-start(bf16[128,16,128]{0,2,1:T(8,128)(2,1)} %multiply_convert_fusion.4) | copy-start | bytes 1572868
  852.5 303.8 %copy-start.37 = (f32[1024]{0:T(1024)S(1)}, f32[1024]{0:T(1024)}, u32[]{:S(2)}) copy-start(f32[1024]{0:T(1024)} %param.28) | copy-start | bytes 12292
  852.5 303.8 %copy-start.44 = (f32[128]{0:T(128)S(1)}, f32[128]{0:T(128)}, u32[]{:S(2)}) copy-start(f32[128]{0:T(128)} %copy-done.43) | copy-start | bytes 1540
  1167.9 239.9 %copy-start.20 = (bf16[128,3072]{1,0:T(8,128)(2,1)S(1)}, bf16[128,3072]{1,0:T(8,128)(2,1)}, u32[]{:S(2)}) copy-start(bf16[128,3072]{1,0:T(8,128)(2,1)} %get-tuple-element.417) | copy-start | bytes 2359300
  1167.9 583.8 %all-reduce.4.cloned.1.call-start = ((), (), s32[]{:S(2)}) async-start(), calls=%async_computation.17 | async-start | bytes 15728640 | tf_op jit(solution)/shard_map/psum | solution.py:302
  1407.9 5.9 copy-start.15
  1407.9 5.9 copy-start.33
  1407.9 6.7 copy-start.16
  1751.8 5.9 slice-start
  1751.8 4.4 copy-start.12
  1751.8 5.9 slice-start.1
  (30 other events, 82.8 us)
Sparse Core Ops, SparseCore 0:
  9.7 29.2 all-gather.9
  40.6 25.9 all-gather.13
  68.3 37.8 all-gather.17
  108.3 166.1 all-gather.11
  276.5 168.2 all-gather.15
  446.3 39.9 all-gather.19
  488.0 49.7 all-gather.21
  539.5 49.7 all-gather.23
  590.9 49.7 all-gather.25
  797.5 178.7 reduce-scatter.4
  978.7 174.6 reduce-scatter.6
  1156.0 143.5 reduce-scatter.10
  1302.5 105.3 reduce-scatter.8
  1410.5 341.2 all-reduce.3
where the time goes:
time: 1770 us
  waiting for transfers between devices  1260 us (71%)
  matrix products  211 us (12%)
  local copies, waits for them, and re-layouts  132 us (7%)
  other arithmetic  75 us (4%)
  blocking collectives  68.6 us (4%)
    psum x1, waiting for transfers between devices, shards(): lax.psum(attn_sum.astype(jnp.bfloat16), 'ctx').astype(jnp.float32)  264 us
    reduce_scatter x1, waiting for transfers between devices, shards(): lax.psum_scatter(value_cots.reshape(seq_len, key_cols).astype(jnp.bfloat1...  176 us
    all_gather x1, waiting for transfers between devices, shards(): lax.all_gather(key_rot, 'ctx', axis=0, tiled=True)  161 us
    all_gather x1, waiting for transfers between devices, shards(): lax.all_gather(value_rows, 'ctx', axis=0, tiled=True)  157 us
    reduce_scatter x1, waiting for transfers between devices, shards(): lax.psum_scatter(jnp.concatenate([matmul_cols(mlp_in, gate_up_cot), matmu...  131 us
    reduce_scatter x1, waiting for transfers between devices, shards(): lax.psum_scatter((key_cots.reshape(seq_len, key_cols) * score_scale).asty...  124 us
    reduce_scatter x1, waiting for transfers between devices, shards(): lax.psum_scatter(jnp.concatenate([matmul_cols(attn_in, proj_cot), matmul_...  108 us
    psum x1, blocking collectives, shards(): lax.psum((attn_gain_part, mlp_gain_part, query_gain_part, key_gain_part),...  68.6 us
  transfers between devices with their start and end apart: 14, of which 12 were waited for; matrix products, arithmetic and copies ran while one was open for 14% of the time, Pallas kernels for 0%

commit v1 on v0

v1 whole, which is shorter than its diff:
```python
import functools

import jax
import jax.numpy as jnp
from jax import lax
from jax.experimental import pallas as pl
from jax.experimental.pallas import tpu as pltpu
from jax.sharding import PartitionSpec as P

EPSILON = 1e-06
ROPE_BASE = 1000000.0
MESH = pl.DeviceIdType.MESH
HBM = pl.BlockSpec(memory_space=pltpu.HBM)
VMEM = pl.BlockSpec(memory_space=pltpu.VMEM)
SMEM = pl.BlockSpec(memory_space=pltpu.SMEM)
LOG2E = 1.4426950408889634
VMEM_LIMIT = 56 * 1024 * 1024
BF16 = jnp.bfloat16
F32 = jnp.float32


class Spot:
    def __init__(self, a, b, zl, zh, core):
        self.a, self.b, self.zl, self.zh, self.core = a, b, zl, zh, core

    def move(self, a=None, b=None, zl=None, zh=None):
        return Spot(
            self.a if a is None else a,
            self.b if b is None else b,
            self.zl if zl is None else zl,
            self.zh if zh is None else zh,
            self.core,
        )

    def id(self):
        first = self.core == 0
        x = jnp.where(first, self.a, self.b)
        y = jnp.where(first, self.b, self.a)
        return (self.zl * 16 + y * 4 + x, self.zh * 2 + self.core)

    def sibling(self):
        return Spot(self.b, self.a, self.zl, self.zh, 1 - self.core)

    def across(self):
        return self.move(zl=1 - self.zl, zh=1 - self.zh)


def here():
    ctx = lax.axis_index("ctx")
    fsdp = lax.axis_index("fsdp")
    x = lax.rem(ctx, 4)
    y = lax.rem(ctx // 4, 4)
    core = lax.rem(fsdp, 2)
    first = core == 0
    return Spot(jnp.where(first, x, y), jnp.where(first, y, x), ctx // 16, fsdp // 2, core)


def ring(position, step):
    return lax.rem(position + step + 4, 4)


def greet(spots):
    barrier = pltpu.get_barrier_semaphore()
    for spot in spots:
        pl.semaphore_signal(barrier, inc=1, device_id=spot.id(), device_id_type=MESH)
    pl.semaphore_wait(barrier, len(spots))


def remote(src, dst, send_sem, recv_sem, spot):
    return pltpu.make_async_remote_copy(
        src_ref=src,
        dst_ref=dst,
        send_sem=send_sem,
        recv_sem=recv_sem,
        device_id=spot.id(),
        device_id_type=MESH,
    )


def comm_params(collective_id):
    return pltpu.CompilerParams(
        collective_id=collective_id, has_side_effects=True, vmem_limit_bytes=VMEM_LIMIT
    )


def gather_body(count, *refs):
    ins, outs = refs[:count], refs[count : 2 * count]
    send, recv, local_sem = refs[2 * count :]
    me = here()
    mine = me.zh * 2 + me.core
    other = (1 - me.zh) * 2 + me.core
    twin_mine = me.zh * 2 + 1 - me.core
    twin_other = (1 - me.zh) * 2 + 1 - me.core
    twin, across = me.sibling(), me.across()
    a_next, a_prev = me.move(a=ring(me.a, 1)), me.move(a=ring(me.a, -1))
    b_next, b_prev = me.move(b=ring(me.b, 1)), me.move(b=ring(me.b, -1))
    greet([twin, across, a_next, a_prev, b_next, b_prev])
    sent = []

    def piece(m, a, half=None):
        rows = pl.ds(pl.multiple_of((me.b * 4 + a) * 16, 16), 16)
        return cut(m, rows, half)

    def block(m, b, half=None):
        rows = pl.ds(pl.multiple_of(b * 64, 64), 64)
        return cut(m, rows, half)

    def cut(m, rows, half):
        width = ins[m].shape[1] // 2
        if half is None:
            return outs[m].at[other, rows]
        return outs[m].at[other, rows, pl.ds(half * width, width)]

    def push(m, slot, src, dst, spot):
        copy = remote(src, dst, send.at[m, slot], recv.at[m, slot], spot)
        copy.start()
        sent.append(copy)

    def await_in(m, slot, dst):
        remote(dst, dst, send.at[m, slot], recv.at[m, slot], twin).wait_recv()

    for m in range(count):
        rows = pl.ds(pl.multiple_of((me.b * 4 + me.a) * 16, 16), 16)
        push(m, 0, ins[m].at[rows], outs[m].at[mine, rows], across)
    locals_ = []
    for m in range(count):
        push(m, 9, ins[m], outs[m].at[mine], twin)
        copy = pltpu.make_async_copy(ins[m], outs[m].at[mine], local_sem.at[m])
        copy.start()
        locals_.append(copy)
    for m in range(count):
        await_in(m, 0, piece(m, me.a))
        push(m, 1, piece(m, me.a), piece(m, me.a), a_next)
        push(m, 2, piece(m, me.a), piece(m, me.a), a_prev)

    def stage_a(m):
        left, right, far = ring(me.a, -1), ring(me.a, 1), ring(me.a, 2)
        await_in(m, 1, piece(m, left))
        push(m, 3, piece(m, left, 0), piece(m, left, 0), a_next)
        await_in(m, 2, piece(m, right))
        push(m, 4, piece(m, right, 1), piece(m, right, 1), a_prev)

    def stage_b(m):
        far = ring(me.a, 2)
        await_in(m, 3, piece(m, far, 0))
        await_in(m, 4, piece(m, far, 1))
        push(m, 5, block(m, me.b), block(m, me.b), b_next)
        push(m, 6, block(m, me.b), block(m, me.b), b_prev)
        push(m, 10, block(m, me.b), block(m, me.b), twin)

    def stage_c(m):
        left, right = ring(me.b, -1), ring(me.b, 1)
        await_in(m, 5, block(m, left))
        push(m, 7, block(m, left, 0), block(m, left, 0), b_next)
        push(m, 11, block(m, left), block(m, left), twin)
        await_in(m, 6, block(m, right))
        push(m, 8, block(m, right, 1), block(m, right, 1), b_prev)
        push(m, 12, block(m, right), block(m, right), twin)

    def stage_d(m):
        far = ring(me.b, 2)
        await_in(m, 7, block(m, far, 0))
        await_in(m, 8, block(m, far, 1))
        push(m, 13, block(m, far), block(m, far), twin)

    stages = (stage_a, stage_b, stage_c, stage_d)
    for step in range(count + len(stages) - 1):
        for depth, stage in enumerate(stages):
            if 0 <= step - depth < count:
                stage(step - depth)

    def twin_block(m, b):
        return outs[m].at[twin_other, pl.ds(pl.multiple_of(b * 64, 64), 64)]

    for m in range(count):
        await_in(m, 9, outs[m].at[twin_mine])
        for slot, step in ((10, 0), (11, -1), (12, 1), (13, 2)):
            await_in(m, slot, twin_block(m, ring(me.a, step)))
    for copy in locals_:
        copy.wait()
    for copy in sent:
        copy.wait_send()


def gather_weights(weights):
    count = len(weights)
    outs = pl.pallas_call(
        functools.partial(gather_body, count),
        out_shape=[jax.ShapeDtypeStruct((4,) + w.shape, w.dtype) for w in weights],
        in_specs=[HBM] * count,
        out_specs=[HBM] * count,
        scratch_shapes=[
            pltpu.SemaphoreType.DMA((count, 14)),
            pltpu.SemaphoreType.DMA((count, 14)),
            pltpu.SemaphoreType.DMA((count,)),
        ],
        compiler_params=comm_params(1),
        name="weight_gather",
    )(*weights)
    return [out.reshape(4 * out.shape[1], out.shape[2]) for out in outs]


def group_spot(me, head):
    return me.move(a=lax.rem(head, 4), zl=head // 4)


def swap_body(src, dst, send, recv, local_sem):
    me = here()
    head = me.a + 4 * me.zl
    peers = [lax.rem(head + k, 8) for k in range(1, 8)]
    greet([group_spot(me, peer) for peer in peers])
    own = pltpu.make_async_copy(src.at[head], dst.at[head], local_sem)
    own.start()
    copies = []
    for k, peer in enumerate(peers):
        copy = remote(src.at[peer], dst.at[head], send.at[k], recv.at[k], group_spot(me, peer))
        copy.start()
        copies.append(copy)
    own.wait()
    for k in range(7):
        origin = lax.rem(head + 7 - k, 8)
        remote(src.at[head], dst.at[origin], send.at[k], recv.at[k], group_spot(me, origin)).wait_recv()
    for copy in copies:
        copy.wait_send()


def swap_heads(parts, collective_id):
    return pl.pallas_call(
        swap_body,
        out_shape=jax.ShapeDtypeStruct(parts.shape, parts.dtype),
        in_specs=[HBM],
        out_specs=HBM,
        scratch_shapes=[
            pltpu.SemaphoreType.DMA((7,)),
            pltpu.SemaphoreType.DMA((7,)),
            pltpu.SemaphoreType.DMA,
        ],
        compiler_params=comm_params(collective_id),
        name="head_swap",
    )(parts)


def spread_body(src, rows_out, kv_out, send, recv, kv_send, kv_recv, local_sem):
    me = here()
    head = me.a + 4 * me.zl
    peers = [lax.rem(head + k, 8) for k in range(1, 8)]
    others = [me.move(b=ring(me.b, d)) for d in (1, 2, 3)]
    greet([group_spot(me, peer) for peer in peers] + others)
    sent = []
    for k, peer in enumerate(peers):
        copy = remote(src.at[peer], rows_out.at[head], send.at[k], recv.at[k], group_spot(me, peer))
        copy.start()
        sent.append(copy)
    own = pltpu.make_async_copy(src.at[head], rows_out.at[head], local_sem.at[8])
    own.start()
    locals_ = [own]

    def kv_part(ref):
        return ref.at[:, pl.ds(256, 256)]

    def pass_on(slot, origin, part):
        keep = pltpu.make_async_copy(part, kv_out.at[me.b, origin], local_sem.at[slot])
        keep.start()
        locals_.append(keep)
        for d in range(3):
            copy = remote(
                part, kv_out.at[me.b, origin], kv_send.at[slot, d], kv_recv.at[slot, d], others[d]
            )
            copy.start()
            sent.append(copy)

    pass_on(7, head, kv_part(src.at[head]))
    for k in range(7):
        origin = lax.rem(head + 7 - k, 8)
        remote(
            src.at[head], rows_out.at[origin], send.at[k], recv.at[k], group_spot(me, origin)
        ).wait_recv()
        pass_on(k, origin, kv_part(rows_out.at[origin]))
    for slot in (7, 0, 1, 2, 3, 4, 5, 6):
        origin = head if slot == 7 else lax.rem(head + 7 - slot, 8)
        for d in range(3):
            land = kv_out.at[ring(me.b, -d - 1), origin]
            remote(land, land, kv_send.at[slot, d], kv_recv.at[slot, d], others[d]).wait_recv()
    for copy in locals_:
        copy.wait()
    for copy in sent:
        copy.wait_send()


def spread_rows(parts):
    return pl.pallas_call(
        spread_body,
        out_shape=[
            jax.ShapeDtypeStruct((8, 128, 512), BF16),
            jax.ShapeDtypeStruct((4, 8, 128, 256), BF16),
        ],
        in_specs=[HBM],
        out_specs=[HBM, HBM],
        scratch_shapes=[
            pltpu.SemaphoreType.DMA((7,)),
            pltpu.SemaphoreType.DMA((7,)),
            pltpu.SemaphoreType.DMA((8, 3)),
            pltpu.SemaphoreType.DMA((8, 3)),
            pltpu.SemaphoreType.DMA((9,)),
        ],
        compiler_params=comm_params(2),
        name="qkv_spread",
    )(parts)


def collect_body(dq, dkv, dq_out, dkv_out, held, own, total, q_send, q_recv, p_send, p_recv, t_send, t_recv, local_sem):
    me = here()
    head = me.a + 4 * me.zl
    peers = [lax.rem(head + k, 8) for k in range(1, 8)]
    others = [me.move(b=ring(me.b, d)) for d in (1, 2, 3)]
    greet([group_spot(me, peer) for peer in peers] + others)
    load = pltpu.make_async_copy(dkv.at[me.b], own, local_sem.at[0])
    load.start()
    order = [lax.rem(head + k, 8) for k in (1, 2, 3, 4, 5, 6, 7, 0)]
    sent = []
    for k, peer in enumerate(order):
        for d in range(3):
            copy = remote(
                dkv.at[ring(me.b, d + 1), peer], held.at[d, peer], p_send.at[k, d], p_recv.at[k, d], others[d]
            )
            copy.start()
            sent.append(copy)
    keep = pltpu.make_async_copy(dq.at[head], dq_out.at[head], local_sem.at[1])
    keep.start()
    for k, peer in enumerate(peers):
        copy = remote(dq.at[peer], dq_out.at[head], q_send.at[k], q_recv.at[k], group_spot(me, peer))
        copy.start()
        sent.append(copy)
    load.wait()
    for k, peer in enumerate(order):
        for d in range(3):
            land = held.at[d, peer]
            remote(land, land, p_send.at[k, d], p_recv.at[k, d], others[d]).wait_recv()
        total[peer] = (
            own[peer].astype(F32)
            + held[0, peer].astype(F32)
            + held[1, peer].astype(F32)
            + held[2, peer].astype(F32)
        ).astype(BF16)
        if k < 7:
            copy = remote(total.at[peer], dkv_out.at[head], t_send.at[k], t_recv.at[k], group_spot(me, peer))
            copy.start()
            sent.append(copy)
    mine = pltpu.make_async_copy(total.at[head], dkv_out.at[head], local_sem.at[2])
    mine.start()
    keep.wait()
    mine.wait()
    for k in range(7):
        origin = lax.rem(head + 7 - k, 8)
        remote(dq.at[head], dq_out.at[origin], q_send.at[k], q_recv.at[k], group_spot(me, origin)).wait_recv()
        remote(total.at[head], dkv_out.at[origin], t_send.at[k], t_recv.at[k], group_spot(me, origin)).wait_recv()
    for copy in sent:
        copy.wait_send()


def collect_rows(dq, dkv):
    dma = pltpu.SemaphoreType.DMA
    return pl.pallas_call(
        collect_body,
        out_shape=[
            jax.ShapeDtypeStruct((8, 128, 256), BF16),
            jax.ShapeDtypeStruct((8, 128, 256), BF16),
        ],
        in_specs=[HBM, HBM],
        out_specs=[HBM, HBM],
        scratch_shapes=[
            pltpu.VMEM((3, 8, 128, 256), BF16),
            pltpu.VMEM((8, 128, 256), BF16),
            pltpu.VMEM((8, 128, 256), BF16),
            dma((7,)),
            dma((7,)),
            dma((8, 3)),
            dma((8, 3)),
            dma((7,)),
            dma((7,)),
            dma((3,)),
        ],
        compiler_params=comm_params(3),
        name="qkv_collect",
    )(dq, dkv)


TILE = 512
TILE_BLOCKS = TILE // 64


def dot_nt(left, right):
    return lax.dot_general(left, right, (((1,), (1,)), ((), ())), preferred_element_type=F32)


def dot_nn(left, right):
    return lax.dot_general(left, right, (((1,), (0,)), ((), ())), preferred_element_type=F32)


def stack_heads(rows):
    return jnp.concatenate(
        [rows[:64, :128], rows[:64, 128:256], rows[64:, :128], rows[64:, 128:256]], axis=0
    )


def unstack_heads(stacked):
    return jnp.concatenate(
        [
            jnp.concatenate([stacked[:64], stacked[64:128]], axis=1),
            jnp.concatenate([stacked[128:192], stacked[192:]], axis=1),
        ],
        axis=0,
    )


def sort_rows(order, kv, keys, values):
    @pl.loop(0, 32)
    def _(i):
        low = order[i]
        j, s = i // 8, lax.rem(i, 8)
        rows = kv[j, s]
        at_low = pl.ds(pl.multiple_of(low * 64, 64), 64)
        at_high = pl.ds(pl.multiple_of((63 - low) * 64, 64), 64)
        keys[at_low, :] = rows[:64, :128]
        keys[at_high, :] = rows[64:, :128]
        values[at_low, :] = rows[:64, 128:]
        values[at_high, :] = rows[64:, 128:]


def query_limits(low, columns, start):
    column = lax.broadcasted_iota(jnp.int32, (1, columns), 1) + start
    block = jnp.where(column < 128, low, 63 - low)
    return block * 64 + lax.rem(column, 64)


def mix_body(order, own_order, rows, kv, out, mixed_t, log_total, keys, values, values_t, acc, total):
    sort_rows(order, kv, keys, values)

    @pl.loop(0, 4096 // TILE)
    def _(t):
        at = pl.ds(pl.multiple_of(t * TILE, TILE), TILE)
        values_t[t] = values[at, :].T

    scale = LOG2E * 128.0**-0.5

    @pl.loop(0, 8)
    def _(s):
        low = own_order[s]
        queries = stack_heads(rows[s, :, :256])
        acc[...] = jnp.zeros_like(acc)
        total[...] = jnp.zeros_like(total)

        def tile_step(t, start):
            width = 256 - start
            at = pl.ds(pl.multiple_of(t * TILE, TILE), TILE)
            scores = dot_nt(keys[at, :], queries[start:])
            key_pos = lax.broadcasted_iota(jnp.int32, (TILE, width), 0)
            allowed = key_pos <= query_limits(low, width, start) - t * TILE
            probs = jnp.where(allowed, jnp.exp2(scores * scale), 0.0)
            total[:, start:] += jnp.sum(probs.reshape(TILE // 8, 8, width), axis=0)
            acc[:, start:] += dot_nn(values_t[t], probs.astype(BF16))

        split = low // TILE_BLOCKS + 1
        end = (63 - low) // TILE_BLOCKS + 1

        @pl.loop(0, split)
        def _(t):
            tile_step(t, 0)

        @pl.loop(split, end)
        def _(t):
            tile_step(t, 128)

        full = jnp.sum(total[...], axis=0, keepdims=True)
        mixed = acc[...] / full
        mixed_t[s] = mixed
        log_total[s] = jnp.broadcast_to(jnp.log2(full), (8, 256))
        out[s] = unstack_heads(mixed.T).astype(BF16)


def attention_mix(order, own_order, rows, kv):
    return pl.pallas_call(
        mix_body,
        out_shape=[
            jax.ShapeDtypeStruct((8, 128, 256), BF16),
            jax.ShapeDtypeStruct((8, 128, 256), F32),
            jax.ShapeDtypeStruct((8, 8, 256), F32),
        ],
        in_specs=[SMEM, SMEM, VMEM, VMEM],
        out_specs=[VMEM, VMEM, VMEM],
        scratch_shapes=[
            pltpu.VMEM((4096, 128), BF16),
            pltpu.VMEM((4096, 128), BF16),
            pltpu.VMEM((4096 // TILE, 128, TILE), BF16),
            pltpu.VMEM((128, 256), F32),
            pltpu.VMEM((8, 256), F32),
        ],
        compiler_params=pltpu.CompilerParams(vmem_limit_bytes=VMEM_LIMIT),
        name="attention_mix",
    )(order, own_order, rows, kv)


def grad_body(
    order, own_order, rows, kv, mixed_t, log_total, cots, dq, dkv,
    keys, values, keys_t, key_grad, value_grad, acc,
):
    sort_rows(order, kv, keys, values)

    @pl.loop(0, 4096 // TILE)
    def _(t):
        at = pl.ds(pl.multiple_of(t * TILE, TILE), TILE)
        keys_t[t] = keys[at, :].T

    key_grad[...] = jnp.zeros_like(key_grad)
    value_grad[...] = jnp.zeros_like(value_grad)
    scale = LOG2E * 128.0**-0.5

    @pl.loop(0, 8)
    def _(s):
        low = own_order[s]
        queries = stack_heads(rows[s, :, :256])
        cot = stack_heads(cots[s])
        delta = jnp.sum(cot.astype(F32).T * mixed_t[s], axis=0, keepdims=True)
        logs = log_total[s, 0:1, :]
        acc[...] = jnp.zeros_like(acc)

        def tile_step(t, start):
            width = 256 - start
            at = pl.ds(pl.multiple_of(t * TILE, TILE), TILE)
            scores = dot_nt(keys[at, :], queries[start:])
            prob_cot = dot_nt(values[at, :], cot[start:])
            key_pos = lax.broadcasted_iota(jnp.int32, (TILE, width), 0)
            allowed = key_pos <= query_limits(low, width, start) - t * TILE
            probs = jnp.where(allowed, jnp.exp2(scores * scale - logs[:, start:]), 0.0)
            score_cot = (probs * (prob_cot - delta[:, start:])).astype(BF16)
            value_grad[at, :] += dot_nn(probs.astype(BF16), cot[start:])
            key_grad[at, :] += dot_nn(score_cot, queries[start:])
            acc[:, start:] += dot_nn(keys_t[t], score_cot)

        split = low // TILE_BLOCKS + 1
        end = (63 - low) // TILE_BLOCKS + 1

        @pl.loop(0, split)
        def _(t):
            tile_step(t, 0)

        @pl.loop(split, end)
        def _(t):
            tile_step(t, 128)

        dq[s] = unstack_heads((acc[...] * 128.0**-0.5).T).astype(BF16)

    @pl.loop(0, 32)
    def _(i):
        low = order[i]
        j, s = i // 8, lax.rem(i, 8)
        for first, block in ((0, low), (64, 63 - low)):
            at = pl.ds(pl.multiple_of(block * 64, 64), 64)
            dkv[j, s, pl.ds(first, 64), 0:128] = (key_grad[at, :] * 128.0**-0.5).astype(BF16)
            dkv[j, s, pl.ds(first, 64), 128:256] = value_grad[at, :].astype(BF16)


def attention_grad(order, own_order, rows, kv, mixed_t, log_total, cots):
    return pl.pallas_call(
        grad_body,
        out_shape=[
            jax.ShapeDtypeStruct((8, 128, 256), BF16),
            jax.ShapeDtypeStruct((4, 8, 128, 256), BF16),
        ],
        in_specs=[SMEM, SMEM] + [VMEM] * 5,
        out_specs=[VMEM, VMEM],
        scratch_shapes=[
            pltpu.VMEM((4096, 128), BF16),
            pltpu.VMEM((4096, 128), BF16),
            pltpu.VMEM((4096 // TILE, 128, TILE), BF16),
            pltpu.VMEM((4096, 128), F32),
            pltpu.VMEM((4096, 128), F32),
            pltpu.VMEM((128, 256), F32),
        ],
        compiler_params=pltpu.CompilerParams(vmem_limit_bytes=VMEM_LIMIT),
        name="attention_grad",
    )(order, own_order, rows, kv, mixed_t, log_total, cots)


def reduce_body(chunks, count, *refs):
    ins, gains = refs[:count], refs[count]
    outs, gains_out = refs[count + 1 : 2 * count + 1], refs[2 * count + 1]
    scratch = refs[2 * count + 2 :]
    per_chunk = 15
    send, recv, load, gain_slots, gain_send, gain_recv = scratch[per_chunk * len(chunks) :]
    me = here()
    twin, across = me.sibling(), me.across()
    a_next, a_prev = me.move(a=ring(me.a, 1)), me.move(a=ring(me.a, -1))
    b_next, b_prev = me.move(b=ring(me.b, 1)), me.move(b=ring(me.b, -1))
    z_low = me.move(zl=1 - me.zl)
    a_far, b_far = me.move(a=ring(me.a, 2)), me.move(b=ring(me.b, 2))
    z_high = me.move(zh=1 - me.zh)
    greet([twin, across, a_next, a_prev, b_next, b_prev, z_low, a_far, b_far, z_high])
    sent = []

    def push(k, slot, src, dst, spot):
        copy = remote(src, dst, send.at[k, slot], recv.at[k, slot], spot)
        copy.start()
        sent.append(copy)

    def await_in(k, slot, dst):
        remote(dst, dst, send.at[k, slot], recv.at[k, slot], twin).wait_recv()

    def names(k):
        which, start, width = chunks[k]
        return ins[which], outs[which], start, width, scratch[per_chunk * k : per_chunk * (k + 1)]

    def big(ref, start, width, b, half=None):
        rows = pl.ds(pl.multiple_of(b * 64, 64), 64)
        if half is None:
            return ref.at[:, rows, pl.ds(start, width)]
        return ref.at[:, rows, pl.ds(start + half * (width // 2), width // 2)]

    def small(ref, width, a, half=None):
        rows = pl.ds(pl.multiple_of(a * 16, 16), 16)
        if half is None:
            return ref.at[:, rows]
        return ref.at[:, rows, pl.ds(half * (width // 2), width // 2)]

    def add_rows(dst, sources, rows):
        for zh in range(2):

            @pl.loop(0, rows // 16)
            def _(r):
                at = pl.ds(pl.multiple_of(r * 16, 16), 16)
                total = sources[0][zh, at].astype(F32)
                for source in sources[1:]:
                    total = total + source[zh, at].astype(F32)
                dst[zh, at] = total.astype(BF16)

    loads = {}

    def step0(k):
        src, _, start, width, bufs = names(k)
        far_a, far_b, in_a, in_b, own_a, own_b, own, sum1 = bufs[:8]
        left, right, far = ring(me.b, -1), ring(me.b, 1), ring(me.b, 2)
        half = width // 2
        push(k, 0, big(src, start, width, far, 0), far_a, b_next)
        push(k, 1, big(src, start, width, far, 1), far_b, b_prev)
        push(k, 2, big(src, start, width, right, 1), in_a.at[:, :, pl.ds(half, half)], b_next)
        push(k, 3, big(src, start, width, left, 0), in_b.at[:, :, pl.ds(0, half)], b_prev)
        items = (
            (big(src, start, width, right, 0), own_a),
            (big(src, start, width, left, 1), own_b),
            (big(src, start, width, me.b), own),
        )
        for i, (source, target) in enumerate(items):
            copy = pltpu.make_async_copy(source, target, load.at[k, i])
            copy.start()
            loads[k, i] = copy

    def step1(k):
        _, _, _, width, bufs = names(k)
        far_a, far_b, in_a, in_b, own_a, own_b, own, sum1 = bufs[:8]
        half = width // 2
        await_in(k, 0, far_a)
        loads[k, 0].wait()
        add_rows(own_a, [own_a, far_a], 64)
        push(k, 4, own_a, in_a.at[:, :, pl.ds(0, half)], b_next)
        await_in(k, 1, far_b)
        loads[k, 1].wait()
        add_rows(own_b, [own_b, far_b], 64)
        push(k, 5, own_b, in_b.at[:, :, pl.ds(half, half)], b_prev)

    def step2(k):
        _, _, _, width, bufs = names(k)
        far_a, far_b, in_a, in_b, own_a, own_b, own, sum1 = bufs[:8]
        far2_a, far2_b, in2_a, in2_b = bufs[8:12]
        half = width // 2
        loads[k, 2].wait()
        await_in(k, 2, in_a.at[:, :, pl.ds(half, half)])
        await_in(k, 4, in_a.at[:, :, pl.ds(0, half)])
        await_in(k, 3, in_b.at[:, :, pl.ds(0, half)])
        await_in(k, 5, in_b.at[:, :, pl.ds(half, half)])
        add_rows(sum1, [own, in_a, in_b], 64)
        left, right, far = ring(me.a, -1), ring(me.a, 1), ring(me.a, 2)
        push(k, 6, small(sum1, width, far, 0), far2_a, a_next)
        push(k, 7, small(sum1, width, far, 1), far2_b, a_prev)
        push(k, 8, small(sum1, width, right, 1), in2_a.at[:, :, pl.ds(half, half)], a_next)
        push(k, 9, small(sum1, width, left, 0), in2_b.at[:, :, pl.ds(0, half)], a_prev)

    def step3(k):
        _, _, _, width, bufs = names(k)
        sum1 = bufs[7]
        far2_a, far2_b, in2_a, in2_b, sum2, from_z, from_low = bufs[8:]
        left, right = ring(me.a, -1), ring(me.a, 1)
        half = width // 2
        await_in(k, 6, far2_a)
        far2_a[...] = (
            far2_a[...].astype(F32)
            + sum1[:, pl.ds(pl.multiple_of(right * 16, 16), 16), pl.ds(0, half)].astype(F32)
        ).astype(BF16)
        push(k, 10, far2_a, in2_a.at[:, :, pl.ds(0, half)], a_next)
        await_in(k, 7, far2_b)
        far2_b[...] = (
            far2_b[...].astype(F32)
            + sum1[:, pl.ds(pl.multiple_of(left * 16, 16), 16), pl.ds(half, half)].astype(F32)
        ).astype(BF16)
        push(k, 11, far2_b, in2_b.at[:, :, pl.ds(half, half)], a_prev)

    def step4(k):
        _, _, _, width, bufs = names(k)
        sum1 = bufs[7]
        far2_a, far2_b, in2_a, in2_b, sum2, from_z, from_low = bufs[8:]
        half = width // 2
        await_in(k, 8, in2_a.at[:, :, pl.ds(half, half)])
        await_in(k, 10, in2_a.at[:, :, pl.ds(0, half)])
        await_in(k, 9, in2_b.at[:, :, pl.ds(0, half)])
        await_in(k, 11, in2_b.at[:, :, pl.ds(half, half)])
        sum2[...] = (
            sum1[:, pl.ds(pl.multiple_of(me.a * 16, 16), 16), :].astype(F32)
            + in2_a[...].astype(F32)
            + in2_b[...].astype(F32)
        ).astype(BF16)
        push(k, 12, sum2.at[1 - me.zh], from_z, across)

    def step5(k):
        _, _, _, width, bufs = names(k)
        far2_a, far2_b, in2_a, in2_b, sum2, from_z, from_low = bufs[8:]
        await_in(k, 12, from_z)
        from_z[...] = (from_z[...].astype(F32) + sum2[me.zh].astype(F32)).astype(BF16)
        push(k, 13, from_z, from_low, z_low)

    def out_cut(ref, start, width, row, rows, half=None):
        at = pl.ds(pl.multiple_of(row, 16), rows)
        if half is None:
            return ref.at[at, pl.ds(start, width)]
        return ref.at[at, pl.ds(start + half * (width // 2), width // 2)]

    def step6(k):
        _, out, start, width, bufs = names(k)
        far2_a, far2_b, in2_a, in2_b, sum2, from_z, from_low = bufs[8:]
        await_in(k, 13, from_low)
        final = in2_a.at[0]
        final[...] = (from_z[...].astype(F32) + from_low[...].astype(F32)).astype(BF16)
        row = (me.b * 4 + me.a) * 16
        place = out_cut(out, start, width, row, 16)
        push(k, 14, final, place, a_next)
        push(k, 15, final, place, a_prev)
        copy = pltpu.make_async_copy(final, place, load.at[k, 3])
        copy.start()
        loads[k, 3] = copy

    def step7(k):
        _, out, start, width, _ = names(k)
        left, right = ring(me.a, -1), ring(me.a, 1)
        row_l, row_r = (me.b * 4 + left) * 16, (me.b * 4 + right) * 16
        await_in(k, 14, out_cut(out, start, width, row_l, 16))
        push(k, 16, out_cut(out, start, width, row_l, 16, 0), out_cut(out, start, width, row_l, 16, 0), a_next)
        await_in(k, 15, out_cut(out, start, width, row_r, 16))
        push(k, 17, out_cut(out, start, width, row_r, 16, 1), out_cut(out, start, width, row_r, 16, 1), a_prev)

    def step8(k):
        _, out, start, width, _ = names(k)
        row_f = (me.b * 4 + ring(me.a, 2)) * 16
        await_in(k, 16, out_cut(out, start, width, row_f, 16, 0))
        await_in(k, 17, out_cut(out, start, width, row_f, 16, 1))
        loads[k, 3].wait()
        mine = out_cut(out, start, width, me.b * 64, 64)
        push(k, 18, mine, mine, b_next)
        push(k, 19, mine, mine, b_prev)

    def step9(k):
        _, out, start, width, _ = names(k)
        row_l, row_r = ring(me.b, -1) * 64, ring(me.b, 1) * 64
        await_in(k, 18, out_cut(out, start, width, row_l, 64))
        push(k, 20, out_cut(out, start, width, row_l, 64, 0), out_cut(out, start, width, row_l, 64, 0), b_next)
        await_in(k, 19, out_cut(out, start, width, row_r, 64))
        push(k, 21, out_cut(out, start, width, row_r, 64, 1), out_cut(out, start, width, row_r, 64, 1), b_prev)

    def step10(k):
        _, out, start, width, _ = names(k)
        row_f = ring(me.b, 2) * 64
        await_in(k, 20, out_cut(out, start, width, row_f, 64, 0))
        await_in(k, 21, out_cut(out, start, width, row_f, 64, 1))

    gain_copies = []
    x_ring = [(me.move(a=ring(me.a, d)), me.move(b=ring(me.b, d))) for d in (1, 2, 3)]
    first = me.core == 0
    x, y = jnp.where(first, me.a, me.b), jnp.where(first, me.b, me.a)
    z = me.zh * 2 + me.zl

    def pick(d, on_x):
        along_a, along_b = x_ring[d - 1]
        use_a = first if on_x else jnp.logical_not(first)
        return Spot(
            jnp.where(use_a, along_a.a, along_b.a),
            jnp.where(use_a, along_a.b, along_b.b),
            me.zl, me.zh, me.core,
        )

    def z_spot(d):
        far = lax.rem(z + d, 4)
        return me.move(zl=lax.rem(far, 2), zh=far // 2)

    def gain_push(stage, slot, position, spots):
        for d, spot in enumerate(spots):
            copy = remote(
                gain_slots.at[stage, position], gain_slots.at[stage, position],
                gain_send.at[stage, d], gain_recv.at[stage, d], spot,
            )
            copy.start()
            gain_copies.append(copy)

    def gain_wait(stage, position, size):
        for d in range(size - 1):
            land = gain_slots.at[stage, lax.rem(position + size - 1 - d, size)]
            remote(land, land, gain_send.at[stage, d], gain_recv.at[stage, d], twin).wait_recv()

    def gain0():
        gain_slots[0, me.core] = gains[...]
        gain_push(0, 0, me.core, [twin])

    def gain1():
        gain_wait(0, me.core, 2)
        gain_slots[1, x] = gain_slots[0, 0] + gain_slots[0, 1]
        gain_push(1, 0, x, [pick(d, True) for d in (1, 2, 3)])

    def gain_sum(stage):
        return (gain_slots[stage, 0] + gain_slots[stage, 1]) + (gain_slots[stage, 2] + gain_slots[stage, 3])

    def gain2():
        gain_wait(1, x, 4)
        gain_slots[2, y] = gain_sum(1)
        gain_push(2, 0, y, [pick(d, False) for d in (1, 2, 3)])

    def gain3():
        gain_wait(2, y, 4)
        gain_slots[3, z] = gain_sum(2)
        gain_push(3, 0, z, [z_spot(d) for d in (1, 2, 3)])

    def gain4():
        gain_wait(3, z, 4)
        gains_out[...] = gain_sum(3)

    steps = (step0, step1, step2, step3, step4, step5, step6, step7, step8, step9, step10)
    gain_steps = {1: gain0, 3: gain1, 5: gain2, 7: gain3, 9: gain4}
    for turn in range(len(chunks) + len(steps) - 1):
        for depth, step in enumerate(steps):
            if 0 <= turn - depth < len(chunks):
                step(turn - depth)
        if turn in gain_steps:
            gain_steps[turn]()
    for copy in sent + gain_copies:
        copy.wait_send()


def reduce_gradients(parts, chunks, gains, collective_id):
    count = len(parts)
    scratch = []
    for _, _, width in chunks:
        half = width // 2
        scratch += [
            pltpu.VMEM((2, 64, half), BF16),
            pltpu.VMEM((2, 64, half), BF16),
            pltpu.VMEM((2, 64, width), BF16),
            pltpu.VMEM((2, 64, width), BF16),
            pltpu.VMEM((2, 64, half), BF16),
            pltpu.VMEM((2, 64, half), BF16),
            pltpu.VMEM((2, 64, width), BF16),
            pltpu.VMEM((2, 64, width), BF16),
            pltpu.VMEM((2, 16, half), BF16),
            pltpu.VMEM((2, 16, half), BF16),
            pltpu.VMEM((2, 16, width), BF16),
            pltpu.VMEM((2, 16, width), BF16),
            pltpu.VMEM((2, 16, width), BF16),
            pltpu.VMEM((16, width), BF16),
            pltpu.VMEM((16, width), BF16),
        ]
    dma = pltpu.SemaphoreType.DMA
    scratch += [
        dma((len(chunks), 22)),
        dma((len(chunks), 22)),
        dma((len(chunks), 4)),
        pltpu.VMEM((4, 4) + gains.shape, F32),
        dma((4, 3)),
        dma((4, 3)),
    ]
    return pl.pallas_call(
        functools.partial(reduce_body, chunks, count),
        out_shape=[jax.ShapeDtypeStruct(part.shape[1:], BF16) for part in parts]
        + [jax.ShapeDtypeStruct(gains.shape, F32)],
        in_specs=[HBM] * count + [VMEM],
        out_specs=[HBM] * count + [VMEM],
        scratch_shapes=scratch,
        compiler_params=comm_params(collective_id),
        name="gradient_reduce",
    )(*parts, gains)


def rms_scale(values):
    return lax.rsqrt(jnp.mean(values * values, axis=-1, keepdims=True) + EPSILON)


def rope_tables(extent, positions):
    frequency = jnp.power(ROPE_BASE, -jnp.arange(0, extent, 2, dtype=F32) / extent)
    angles = positions.astype(F32)[:, None] * frequency[None, :]
    cosine = jnp.concatenate([jnp.cos(angles), jnp.cos(angles)], -1)[:, None, :]
    sine_rows = jnp.concatenate([jnp.sin(angles), jnp.sin(angles)], -1)[:, None, :]
    return cosine, sine_rows


def rotate(values, tables):
    cosine, sine_rows = tables
    half = values.shape[-1] // 2
    turned = jnp.concatenate([-values[..., half:], values[..., :half]], -1)
    return values * cosine + turned * sine_rows


def rotate_back(grads, tables):
    cosine, sine_rows = tables
    half = grads.shape[-1] // 2
    scaled = grads * sine_rows
    return grads * cosine + jnp.concatenate([scaled[..., half:], -scaled[..., :half]], -1)


def norm_back(grad_out, normed, scale_inv):
    return scale_inv * (grad_out - normed * jnp.mean(grad_out * normed, axis=-1, keepdims=True))


def matmul(matrix, second):
    return jnp.dot(matrix, second, preferred_element_type=F32)


def matmul_rows(matrix, second):
    return lax.dot_general(matrix, second, (((1,), (1,)), ((), ())), preferred_element_type=F32)


def twin_swap(value):
    return lax.ppermute(value, "fsdp", [(0, 1), (1, 0), (2, 3), (3, 2)])


def pair_grad(left, right, core):
    tokens = left.shape[0]
    split = left.reshape(tokens, 2, 2, 256)
    keep = lax.dynamic_index_in_dim(split, core, 2, keepdims=False)
    give = lax.dynamic_index_in_dim(split, 1 - core, 2, keepdims=False)
    left_pair = jnp.concatenate([keep, twin_swap(give)], 0).reshape(2 * tokens, 512)
    right_pair = jnp.concatenate([right, twin_swap(right)], 0)
    grad = lax.dot_general(left_pair, right_pair, (((0,), (0,)), ((), ())), preferred_element_type=F32)
    return grad.astype(BF16).reshape(2, 256, right.shape[1])


def shards(
    tokens,
    query_weight,
    key_weight,
    value_weight,
    out_weight,
    gate_weight,
    up_weight,
    down_weight,
    attn_gain,
    mlp_gain,
    query_gain,
    key_gain,
    pair_order,
    out_grad,
):
    inputs = tokens[0].astype(F32)
    rows = inputs.shape[0]
    pair_row = pair_order[0]
    ctx = lax.axis_index("ctx")
    core = lax.rem(lax.axis_index("fsdp"), 2)
    first = lax.dynamic_index_in_dim(pair_row, ctx, 0, keepdims=False)
    inner = jnp.arange(rows, dtype=jnp.int32)
    own_pos = jnp.where(inner < 64, first, 63 - first) * 64 + inner % 64
    tables = rope_tables(128, own_pos)
    spots = pair_row.reshape(2, 4, 4)
    order = jnp.where(core == 0, spots.transpose(1, 0, 2), spots.transpose(2, 0, 1))
    x, y = ctx % 4, (ctx // 4) % 4
    own_order = lax.dynamic_index_in_dim(order, jnp.where(core == 0, y, x), 0, keepdims=False).reshape(8)
    order = order.reshape(32)

    full_query, full_key, full_value, full_out, full_gate, full_up, full_down = gather_weights(
        [query_weight, key_weight, value_weight, out_weight, gate_weight, up_weight, down_weight]
    )
    attn_scale = rms_scale(inputs)
    attn_normed = inputs * attn_scale
    attn_in = (attn_normed * attn_gain).astype(BF16)
    query_raw = matmul(attn_in, full_query).reshape(rows, 16, 128)
    key_raw = matmul(attn_in, full_key).reshape(rows, 8, 128)
    value_rows = matmul(attn_in, full_value).astype(BF16)
    query_inv = rms_scale(query_raw)
    query_hat = query_raw * query_inv
    key_inv = rms_scale(key_raw)
    key_hat = key_raw * key_inv
    query_rot = rotate(query_hat * query_gain, tables).astype(BF16).reshape(rows, 8, 256)
    key_rot = rotate(key_hat * key_gain, tables).astype(BF16)
    packed = jnp.concatenate([query_rot, key_rot, value_rows.reshape(rows, 8, 128)], -1).transpose(1, 0, 2)
    head_rows, head_kv = spread_rows(packed)
    mixed, mixed_t, log_total = attention_mix(order, own_order, head_rows, head_kv)
    attn_out = swap_heads(mixed, 4).transpose(1, 0, 2).reshape(rows, 2048)

    middle = inputs + matmul_rows(attn_out, full_out)
    mlp_scale = rms_scale(middle)
    mlp_normed = middle * mlp_scale
    mlp_in = (mlp_normed * mlp_gain).astype(BF16)
    gate_pre = matmul(mlp_in, full_gate)
    up_pre = matmul(mlp_in, full_up)
    sigmoid_gate = jax.nn.sigmoid(gate_pre)
    silu_gate = gate_pre * sigmoid_gate
    hidden = (silu_gate * up_pre).astype(BF16)
    result = middle + matmul_rows(hidden, full_down)
    down_cot = out_grad[0]
    hidden_cot = matmul(down_cot, full_down)
    gate_cot = (hidden_cot * up_pre * sigmoid_gate * (1.0 + gate_pre * (1.0 - sigmoid_gate))).astype(BF16)
    up_cot = (hidden_cot * silu_gate).astype(BF16)
    mlp_in_cot = matmul_rows(gate_cot, full_gate) + matmul_rows(up_cot, full_up)
    mlp_gain_part = jnp.sum(mlp_in_cot * mlp_normed, axis=0)
    middle_cot = down_cot.astype(F32) + norm_back(mlp_in_cot * mlp_gain, mlp_normed, mlp_scale)
    branch_cot = middle_cot.astype(BF16)
    attended_cot = matmul(branch_cot, full_out).astype(BF16).reshape(rows, 8, 256).transpose(1, 0, 2)
    head_cots = swap_heads(attended_cot, 4)
    dq, dkv = attention_grad(order, own_order, head_rows, head_kv, mixed_t, log_total, head_cots)
    dq, dkv = collect_rows(dq, dkv)
    query_rot_cot = dq.astype(F32).transpose(1, 0, 2).reshape(rows, 16, 128)
    key_value_cot = dkv.transpose(1, 0, 2)
    value_raw_cot = key_value_cot[..., 128:].reshape(rows, 1024)
    key_hat_cot = rotate_back(key_value_cot[..., :128].astype(F32), tables)
    key_gain_part = jnp.sum(key_hat_cot * key_hat, axis=(0, 1))
    key_raw_cot = norm_back(key_hat_cot * key_gain, key_hat, key_inv).astype(BF16).reshape(rows, 1024)
    query_hat_cot = rotate_back(query_rot_cot, tables)
    query_gain_part = jnp.sum(query_hat_cot * query_hat, axis=(0, 1))
    query_raw_cot = norm_back(query_hat_cot * query_gain, query_hat, query_inv).astype(BF16).reshape(rows, 2048)
    attn_in_cot = (
        matmul_rows(query_raw_cot, full_query)
        + matmul_rows(key_raw_cot, full_key)
        + matmul_rows(value_raw_cot, full_value)
    )
    attn_gain_part = jnp.sum(attn_in_cot * attn_normed, axis=0)
    input_cot = middle_cot + norm_back(attn_in_cot * attn_gain, attn_normed, attn_scale)

    grads = [
        pair_grad(mlp_in, jnp.concatenate([gate_cot, up_cot], 1), core),
        pair_grad(down_cot, hidden, core),
        pair_grad(attn_in, jnp.concatenate([query_raw_cot, key_raw_cot, value_raw_cot], 1), core),
        pair_grad(branch_cot, attn_out, core),
    ]
    gains = jnp.concatenate(
        [attn_gain_part, mlp_gain_part, query_gain_part, key_gain_part, jnp.zeros(768, F32)]
    ).reshape(24, 128)
    chunks = ((0, 0, 3072), (0, 3072, 3072), (1, 0, 3072), (2, 0, 4096), (3, 0, 2048))
    gate_up, down, qkv, out, gains = reduce_gradients(grads, chunks, gains, 5)
    gate_up, down, qkv, out = (value.astype(F32) for value in (gate_up, down, qkv, out))
    gains = gains.reshape(-1)
    return (
        result.astype(BF16)[None],
        input_cot[None],
        qkv[:, :2048],
        qkv[:, 2048:3072],
        qkv[:, 3072:],
        out,
        gate_up[:, :3072],
        gate_up[:, 3072:],
        down,
        gains[:1024],
        gains[1024:2048],
        gains[2048:2176],
        gains[2176:2304],
    )


def solution(mesh):
    rows, split, whole = P("fsdp", None), P("fsdp", "ctx", None), P()
    return jax.shard_map(
        shards,
        mesh=mesh,
        in_specs=(split,) + (rows,) * 7 + (whole,) * 4 + (rows, split),
        out_specs=(split, split) + (rows,) * 7 + (whole,) * 4,
        check_vma=False,
    )
```

time: 1770 us -> 661 us (0.37)
  waiting for transfers between devices: 1260 us -> 0.32 us
  Pallas kernels: 0 us -> 510 us
  matrix products: 211 us -> 57 us
  local copies, waits for them, and re-layouts: 132 us -> 57 us
  blocking collectives: 68.6 us -> 0 us
  other arithmetic: 75 us -> 22.6 us
    reduce_scatter x4 -> x0, waiting for transfers between devices: 539 us -> none  [the longest x1 176 us: shards(): lax.psum_scatter(value_cots.reshape(seq_len, key_cols).astype(jnp.bfloat1...]
    pallas_call x0 -> x8, Pallas kernels: none -> 510 us  [the longest x1 245 us: gather_weights(): pl.pallas_call(functools.partial(gather_body, count), out_shape=[jax.Shap...]
    all_gather x9 -> x0, waiting for transfers between devices: 455 us -> none  [the longest x1 161 us: shards(): lax.all_gather(key_rot, 'ctx', axis=0, tiled=True)]
    psum x1 -> x0, waiting for transfers between devices: 264 us -> none  [shards(): lax.psum(attn_sum.astype(jnp.bfloat16), 'ctx').astype(jnp.float32)]
    dot_general x67 -> x11, matrix products: 190 us -> 35.6 us  [the longest x7 17.9 us: matmul(): return jnp.dot(matrix, second, preferred_element_type=F32)]
    psum x1 -> x0, blocking collectives: 68.6 us -> none  [shards(): lax.psum((attn_gain_part, mlp_gain_part, query_gain_part, key_gain_part),...]
    unnamed x103 -> x138, local copies, waits for them, and re-layouts: 49.3 us -> 10.7 us
    dynamic_slice x48 -> x8, local copies, waits for them, and re-layouts: 33 us -> 4.85 us  [the longest x4 2.51 us: pair_grad(): keep = lax.dynamic_index_in_dim(split, core, 2, keepdims=False)]
  transfers between devices with their start and end apart: 14 -> 8, of which waited for: 12 -> 1; matrix products, arithmetic and copies ran while one was open for 14% -> 9% of each run, Pallas kernels for 0% -> 10%
where the time goes in v1:
time: 661 us; the launch traced here: 652 us
  Pallas kernels  510 us (77%)
  local copies, waits for them, and re-layouts  57 us (9%)
  matrix products  57 us (9%)
  other arithmetic  22.6 us (3%)
    pallas_call x1, Pallas kernels, gather_weights(): pl.pallas_call(functools.partial(gather_body, count), out_shape=[jax.Shap...  245 us
    pallas_call x1, Pallas kernels, reduce_gradients(): pl.pallas_call(functools.partial(reduce_body, chunks, count), out_shape=[...  134 us
    pallas_call x1, Pallas kernels, attention_grad(): pl.pallas_call(grad_body, out_shape=[jax.ShapeDtypeStruct((8, 128, 256),...  31.2 us
    pallas_call x1, Pallas kernels, spread_rows(): pl.pallas_call(spread_body, out_shape=[jax.ShapeDtypeStruct((8, 128, 512)...  27.6 us
    pallas_call x1, Pallas kernels, collect_rows(): pl.pallas_call(collect_body, out_shape=[jax.ShapeDtypeStruct((8, 128, 256...  25.6 us
    pallas_call x1, Pallas kernels, attention_mix(): pl.pallas_call(mix_body, out_shape=[jax.ShapeDtypeStruct((8, 128, 256), B...  25 us
    dot_general x7, matrix products, matmul_rows(): lax.dot_general(matrix, second, (((1,), (1,)), ((), ())), preferred_eleme...  21.4 us
    pallas_call x2, Pallas kernels, swap_heads(): pl.pallas_call(swap_body, out_shape=jax.ShapeDtypeStruct(parts.shape, par...  21.3 us
  transfers between devices with their start and end apart: 8, of which 1 were waited for; matrix products, arithmetic and copies ran while one was open for 9% of the time, Pallas kernels for 10%

profile of v1, /device:TPU:0, one launch (start us, length us, event | category | flops | bytes accessed | tf_op | source)
XLA Modules:
  0.0 651.9 jit_solution(14444393531008483895)
XLA Ops:
  0.7 1.2 constant_dynamic-slice_fusion.8
  5.1 245.4 %weight_gather.1 = (bf16[4,256,2048]{2,1,0:T(8,128)(2,1)}, bf16[4,256,1024]{2,1,0:T(8,128)(2,1)}, bf16[4,256,1024]{2,1,0:T(8,128)(2,1)}, bf16[4,256,2048]{2,1,0:...) custom-call(bf16[256,2048]{1,0:T(8,128)(2,1)} %refs_0_.1, ...), custom_call_target="tpu_custom_call" | custom-call | tf_op jit(solution)/shard_map/weight_gather/pallas_call | solution.py:187
  250.6 6.4 copy.65
  257.2 3.5 multiply_reduce_fusion.2
  261.6 1.1 fusion.20
  262.7 2.0 copy.71
  264.8 2.5 copy.68
  267.3 2.4 multiply_reduce_fusion.8
  270.4 1.1 copy-done.5
  271.5 1.2 convolution_convert_fusion.5
  272.7 1.8 copy.70
  274.6 1.8 copy.72
  276.4 1.0 fusion.26
  277.4 1.1 maximum_bitcast_fusion.src
  278.5 27.6 %qkv_spread.1 = (bf16[8,128,512]{2,1,0:T(8,128)(2,1)}, bf16[4,8,128,256]{3,2,1,0:T(8,128)(2,1)}) custom-call(bf16[8,128,512]{2,1,0:T(8,128)(2,1)} %maximum_bitcast_fusion.src), custom_call_target="tpu_custom_call" | custom-call | tf_op jit(solution)/shard_map/qkv_spread/pallas_call | solution.py:291
  309.0 25.0 %attention_mix.1 = (bf16[8,128,256]{2,1,0:T(8,128)(2,1)}, f32[8,128,256]{2,1,0:T(8,128)}, f32[8,8,256]{2,1,0:T(8,128)}) custom-call(s32[32]{0:T(128)} %reshape.260.order, s32[8]{0:T(128)} %reshape.261.own_order, bf16[8,128,512]{2,1,0:T(8,128)(2,1)} %get-tuple-element.37.rows, bf16[4,8,128,256]{3,2,1,0:T(8,128)(2,1)} %get-tuple-element.38.kv), custom_call_target="tpu_custom_call" | custom-call | tf_op jit(solution)/shard_map/attention_mix/pallas_call | solution.py:482
  334.0 10.6 %head_swap.2 = bf16[8,128,256]{2,1,0:T(8,128)(2,1)} custom-call(bf16[8,128,256]{2,1,0:T(8,128)(2,1)} %get-tuple-element.39.src), custom_call_target="tpu_custom_call" | custom-call | tf_op jit(solution)/shard_map/head_swap/pallas_call | solution.py:228
  344.5 1.3 copy.73
  345.9 4.0 multiply_reduce_fusion.7
  350.0 3.9 fusion.74
  354.8 1.0 fusion.73
  356.0 0.8 slice-done.5
  356.8 2.9 multiply_convert_fusion
  359.7 2.2 fusion.75
  362.0 2.9 multiply_reduce_fusion.4
  364.9 0.8 copy-done.10
  366.0 1.3 constant_dynamic-slice_fusion.1
  368.0 2.9 convolution_convert_fusion.4
  371.2 1.0 copy.76
  372.2 10.8 %head_swap.3.cots = bf16[8,128,256]{2,1,0:T(8,128)(2,1)} custom-call(bf16[8,128,256]{2,1,0:T(8,128)(2,1)} %bitcast.178), custom_call_target="tpu_custom_call" | custom-call | tf_op jit(solution)/shard_map/head_swap/pallas_call | solution.py:228
  383.0 31.2 %attention_grad.1 = (bf16[8,128,256]{2,1,0:T(8,128)(2,1)}, bf16[4,8,128,256]{3,2,1,0:T(8,128)(2,1)}) custom-call(s32[32]{0:T(128)} %reshape.260.order, s32[8]{0:T(128)} %reshape.261.own_order, bf16[8,128,512]{2,1,0:T(8,128)(2,1)} %get-tuple-element.37.rows, bf16[4,8,128,256]{3,2,1,0:T(8,128)(2,1)} %get-tuple-element.38.kv, ...), custom_call_target="tpu_custom_call" | custom-call | tf_op jit(solution)/shard_map/attention_grad/pallas_call | solution.py:564
  414.2 25.6 %qkv_collect.1 = (bf16[8,128,256]{2,1,0:T(8,128)(2,1)}, bf16[8,128,256]{2,1,0:T(8,128)(2,1)}) custom-call(bf16[8,128,256]{2,1,0:T(8,128)(2,1)} %get-tuple-element.46.dq, bf16[4,8,128,256]{3,2,1,0:T(8,128)(2,1)} %get-tuple-element.47.dkv), custom_call_target="tpu_custom_call" | custom-call | tf_op jit(solution)/shard_map/qkv_collect/pallas_call | solution.py:363
  439.8 1.8 convert_multiply_fusion
  441.6 1.7 slice.101
  443.3 2.1 convert_bitcast_fusion
  445.4 1.5 copy.77
  447.8 1.8 multiply_reduce_fusion
  449.8 0.8 copy-done.30
  450.6 0.9 multiply_reduce_fusion.3
  451.5 1.1 multiply_convert_fusion.5
  452.6 1.8 copy.78
  454.4 1.8 copy.79
  457.2 1.0 pad_maximum_fusion.1
  458.3 1.3 reshape.288
  459.5 2.0 copy.86
  461.6 1.2 multiply_convert_fusion.4
  463.5 0.8 copy.88
  464.8 1.3 pad_maximum_fusion
  466.6 3.2 fusion.77
  470.0 6.1 fusion.18
  476.1 0.8 fusion.76
  477.1 2.2 fusion.36
  479.4 1.1 fusion.35
  485.4 1.0 copy.92
  486.8 3.1 convolution_convert_fusion.3
  490.0 4.1 convolution_convert_fusion.2
  494.1 4.7 convolution_convert_fusion.1
  498.8 5.9 convolution_convert_fusion
  504.6 134.2 %gradient_reduce.1 = (bf16[256,6144]{1,0:T(8,128)(2,1)}, bf16[256,3072]{1,0:T(8,128)(2,1)}, bf16[256,4096]{1,0:T(8,128)(2,1)}, bf16[256,2048]{1,0:T(8,128)(2,1)}, f32[24,128]{1,0:T(8,128)}) custom-call(bf16[2,256,6144]{2,1,0:T(8,128)(2,1)} %bitcast.164, bf16[2,256,3072]{2,1,0:T(8,128)(2,1)} %bitcast.152, bf16[2,256,4096]{2,1,0:T(8,128)(2,1)} %bitcast.168, ...), custom_call_target="tpu_custom_call" | custom-call | tf_op jit(solution)/shard_map/gradient_reduce/pallas_call | solution.py:884
  638.8 2.9 fusion.70
  641.7 1.6 slice.102
  644.4 3.5 fusion.69
  647.9 2.0 convert_element_type.132
  650.0 1.6 convert_element_type.130
  (202 shorter events, 20.0 us)
Async XLA Ops:
  250.6 6.5 copy-start
  250.6 6.6 %copy-start.38 = (f32[1024]{0:T(1024)S(1)}, f32[1024]{0:T(1024)}, u32[]{:S(2)}) copy-start(f32[1024]{0:T(1024)} %param.22) | copy-start | bytes 12292
  257.2 10.1 %copy-start.43 = (f32[128]{0:T(128)}, f32[128]{0:T(128)S(1)}, u32[]{:S(2)}) copy-start(f32[128]{0:T(128)S(1)} %add_rsqrt_fusion.3) | copy-start | bytes 1540
  257.2 3.6 copy-start.49
  261.1 3.6 copy-start.3
  267.3 2.6 copy-start.47
  269.9 1.6 copy-start.5
  269.9 1.6 copy-start.44
  272.7 4.7 copy-start.25
  276.4 1.1 copy-start.33
  277.4 29.2 %copy-start.57 = (s32[1,32]{1,0:T(1,128)S(1)}, s32[1,32]{1,0:T(1,128)}, u32[]{:S(2)}) copy-start(s32[1,32]{1,0:T(1,128)} %param.26) | copy-start | bytes 388
  345.8 4.0 copy-start.26
  345.8 4.0 copy-start.40
  349.9 15.0 %copy-start.52 = (f32[128]{0:T(128)}, f32[128]{0:T(128)S(1)}, u32[]{:S(2)}) copy-start(f32[128]{0:T(128)S(1)} %add_rsqrt_fusion.2) | copy-start | bytes 1540
  350.0 4.0 copy-start.7
  350.0 4.1 slice-start.2
  350.0 4.8 slice-start.3
  350.0 5.9 slice-start.4
  354.8 2.0 slice-start.5
  354.8 2.0 copy-start.18
  354.8 7.2 %slice-start = ((s8[6291456]{0:T(1024)(128)(4,1)}), s8[4194304]{0:T(1024)(128)(4,1)S(1)}, s32[]{:S(2)}) async-start(s8[6291456]{0:T(1024)(128)(4,1)} %bitcast.140), calls=%async_computation | async-start | bytes 8388608
  356.8 5.1 slice-start.1
  359.7 2.2 copy-start.13
  359.7 2.2 copy-start.15
  368.0 113.4 %collective-permute-start.6 = (bf16[128,2,256]{2,0,1:T(8,128)(2,1)}, bf16[128,2,256]{2,0,1:T(8,128)(2,1)}, u32[]{:S(2)}, u32[]{:S(2)}) collective-permute-start(bf16[128,2,256]{2,0,1:T(8,128)(2,1)} %bitcast.137), channel_id=1, source_target_pairs={{0,1},{1,0},{2,3},{3,2},{4,5},{5,4},{6,7},{7,6},{8,9},{9,8},{10,11... | collective-permute-start | bytes 393224 | tf_op jit(solution)/shard_map/ppermute | solution.py:935
  441.6 5.4 copy-start.37
  447.8 1.8 copy-start.9
  449.6 1.0 copy-start.30
  449.6 1.0 copy-start.48
  450.6 5.6 copy-start.12
  450.6 5.6 copy-start.51
  456.5 5.1 copy-start.45
  458.3 6.5 %copy-start.14 = (bf16[128,3072]{1,0:T(8,128)(2,1)S(1)}, bf16[128,3072]{1,0:T(8,128)(2,1)}, u32[]{:S(2)}) copy-start(bf16[128,3072]{1,0:T(8,128)(2,1)} %copy-done.13) | copy-start | bytes 2359300
  458.3 6.5 %copy-start.16 = (bf16[128,3072]{1,0:T(8,128)(2,1)S(1)}, bf16[128,3072]{1,0:T(8,128)(2,1)}, u32[]{:S(2)}) copy-start(bf16[128,3072]{1,0:T(8,128)(2,1)} %copy-done.15) | copy-start | bytes 2359300
  458.3 35.8 %collective-permute-start.5 = (bf16[128,4096]{0,1:T(8,128)(2,1)}, bf16[128,4096]{0,1:T(8,128)(2,1)}, u32[]{:S(2)}, u32[]{:S(2)}) collective-permute-start(bf16[128,4096]{0,1:T(8,128)(2,1)} %pad_maximum_fusion.1), channel_id=1, source_target_pairs={{0,1},{1,0},{2,3},{3,2},{4,5},{5,4},{6,7},{7,6},{8,9},{9,8},{10,11... | collective-permute-start | bytes 3145736 | tf_op jit(solution)/shard_map/ppermute | solution.py:935
  462.8 3.7 copy-start.23
  464.3 18.0 %collective-permute-start.4 = (bf16[128,2,256]{2,0,1:T(8,128)(2,1)}, bf16[128,2,256]{2,0,1:T(8,128)(2,1)S(1)}, u32[]{:S(2)}, u32[]{:S(2)}) collective-permute-start(bf16[128,2,256]{2,0,1:T(8,128)(2,1)} %bitcast.44), channel_id=1, source_target_pairs={{0,1},{1,0},{2,3},{3,2},{4,5},{5,4},{6,7},{7,6},{8,9},{9,8},{10,11... | collective-permute-start | bytes 393224 | tf_op jit(solution)/shard_map/ppermute | solution.py:935
  464.8 25.2 %collective-permute-start.3 = (bf16[128,3072]{1,0:T(8,128)(2,1)}, bf16[128,3072]{1,0:T(8,128)(2,1)}, u32[]{:S(2)}, u32[]{:S(2)}) collective-permute-start(bf16[128,3072]{1,0:T(8,128)(2,1)} %get-tuple-element.69), channel_id=1, source_target_pairs={{0,1},{1,0},{2,3},{3,2},{4,5},{5,4},{6,7},{7,6},{8,9},{9,8},{10,11... | collective-permute-start | bytes 2359304 | tf_op jit(solution)/shard_map/ppermute | solution.py:935
  466.1 3.7 copy-start.8
  466.1 32.7 %collective-permute-start.1 = (bf16[128,6144]{1,0:T(8,128)(2,1)}, bf16[128,6144]{1,0:T(8,128)(2,1)}, u32[]{:S(2)}, u32[]{:S(2)}) collective-permute-start(bf16[128,6144]{1,0:T(8,128)(2,1)} %pad_maximum_fusion), channel_id=1, source_target_pairs={{0,1},{1,0},{2,3},{3,2},{4,5},{5,4},{6,7},{7,6},{8,9},{9,8},{10,11... | collective-permute-start | bytes 4718600 | tf_op jit(solution)/shard_map/ppermute | solution.py:935
  470.0 6.1 copy-start.4
  470.0 6.1 copy-start.21
  470.0 7.0 %copy-start.1 = (bf16[4,256,2048]{2,1,0:T(8,128)(2,1)S(1)}, bf16[4,256,2048]{2,1,0:T(8,128)(2,1)}, u32[]{:S(2)}) copy-start(bf16[4,256,2048]{2,1,0:T(8,128)(2,1)} %get-tuple-element.34) | copy-start | bytes 12582916
  476.1 1.0 copy-start.28
  477.1 2.3 copy-start.11
  477.1 2.3 copy-start.19
  477.1 2.3 copy-start.41
  477.1 2.3 copy-start.53
  477.1 2.3 copy-start.56
  479.4 3.4 copy-start.46
  480.5 1.0 copy-start.27
  480.5 4.5 copy-start.32
  481.6 5.3 collective-permute-start.7
  482.3 1.5 collective-permute-start.2
  483.8 2.9 collective-permute-start
  485.4 4.6 copy-start.42
  489.9 4.1 copy-start.24
  490.0 4.1 copy-start.39
  494.0 4.7 copy-start.17
  638.8 2.9 copy-start.6
  641.7 1.6 copy-start.54
  641.7 2.7 copy-start.2
  644.4 3.5 copy-start.29
  647.9 2.0 copy-start.31
  (8 other events, 6.9 us)
